TPU v7x, 32 devices: a whole 2x2x4 slice. The times are simulated.
32 devices in a mesh: wide: 8 (over z, x), narrow: 4 (over y, core).
Axes of the slice: x: 2, y: 2, z: 4, core: 2. Of those that a mesh axis runs over, the one named last changes fastest.
Arguments:
- tokens: bfloat16 [32768, 1024], P(('wide', 'narrow')), may hold values from -6 to 6
- cotangent: bfloat16 [32768, 1024], P(('wide', 'narrow')), may hold values from -12 to 12
- seq_length: int32 [32], P(('wide', 'narrow')), may hold values from 128 to 1024, as said below
- first_gain: bfloat16 [1024], P(('wide', 'narrow')), may hold values from 0.25 to 1.75
- first_shift: bfloat16 [1024], P(('wide', 'narrow')), may hold values from -1.5 to 1.5
- query_weight: bfloat16 [1024, 1024], P(('wide', 'narrow')), may hold values from -0.25 to 0.25
- query_bias: bfloat16 [1024], P(('wide', 'narrow')), may hold values from -1.5 to 1.5
- key_weight: bfloat16 [1024, 1024], P(('wide', 'narrow')), may hold values from -0.1875 to 0.1875
- value_weight: bfloat16 [1024, 1024], P(('wide', 'narrow')), may hold values from -0.1875 to 0.1875
- value_bias: bfloat16 [1024], P(('wide', 'narrow')), may hold values from -1.5 to 1.5
- out_weight: bfloat16 [1024, 1024], P(('wide', 'narrow')), may hold values from -0.5 to 0.5
- out_bias: bfloat16 [1024], P(('wide', 'narrow')), may hold values from -1.5 to 1.5
- second_gain: bfloat16 [1024], P(('wide', 'narrow')), may hold values from 0.25 to 1.75
- second_shift: bfloat16 [1024], P(('wide', 'narrow')), may hold values from -1.5 to 1.5
- up_weight: bfloat16 [1024, 4096], P(('wide', 'narrow')), may hold values from -0.1875 to 0.1875
- up_bias: bfloat16 [4096], P(('wide', 'narrow')), may hold values from -1.5 to 1.5
- down_weight: bfloat16 [4096, 1024], P(('wide', 'narrow')), may hold values from -0.09375 to 0.09375
- down_bias: bfloat16 [1024], P(('wide', 'narrow')), may hold values from -1.5 to 1.5
Outputs:
- output: bfloat16 [32768, 1024], P(('wide', 'narrow'))
- grad_tokens: bfloat16 [32768, 1024], P(('wide', 'narrow'))
- grad_first_gain: float32 [1024], P(('wide', 'narrow'))
- grad_first_shift: float32 [1024], P(('wide', 'narrow'))
- grad_query_weight: float32 [1024, 1024], P(('wide', 'narrow'))
- grad_query_bias: float32 [1024], P(('wide', 'narrow'))
- grad_key_weight: float32 [1024, 1024], P(('wide', 'narrow'))
- grad_value_weight: float32 [1024, 1024], P(('wide', 'narrow'))
- grad_value_bias: float32 [1024], P(('wide', 'narrow'))
- grad_out_weight: float32 [1024, 1024], P(('wide', 'narrow'))
- grad_out_bias: float32 [1024], P(('wide', 'narrow'))
- grad_second_gain: float32 [1024], P(('wide', 'narrow'))
- grad_second_shift: float32 [1024], P(('wide', 'narrow'))
- grad_up_weight: float32 [1024, 4096], P(('wide', 'narrow'))
- grad_up_bias: float32 [4096], P(('wide', 'narrow'))
- grad_down_weight: float32 [4096, 1024], P(('wide', 'narrow'))
- grad_down_bias: float32 [1024], P(('wide', 'narrow'))
Inputs may be any that keep to these rules, and one draw needn't show every extreme that they name: `seq_length`: every entry is 128 or 1024; both values occur in every draw.
All inputs are finite; a program needn't handle non-finite values.
Results may differ from a plain program's by a relative error of at most 0.012.
Values may be sent and summed in bfloat16 or wider, within the bound.
A program may use at most 256 MiB of HBM per device.

v0:
```python
import jax
import jax.numpy as jnp
from jax import lax
from jax.sharding import PartitionSpec as P

H = 8
HD = 128


EPSILON = 1e-05


def collect(parts):
    (
        first_gain,
        first_shift,
        query_weight,
        query_bias,
        key_weight,
        value_weight,
        value_bias,
        out_weight,
        out_bias,
        second_gain,
        second_shift,
        up_weight,
        up_bias,
        down_weight,
        down_bias,
    ) = parts
    return (
        lax.all_gather(first_gain, ("wide", "narrow"), axis=0, tiled=True),
        lax.all_gather(first_shift, ("wide", "narrow"), axis=0, tiled=True),
        lax.all_gather(query_weight, ("wide", "narrow"), axis=0, tiled=True),
        lax.all_gather(query_bias, ("wide", "narrow"), axis=0, tiled=True),
        lax.all_gather(key_weight, ("wide", "narrow"), axis=0, tiled=True),
        lax.all_gather(value_weight, ("wide", "narrow"), axis=0, tiled=True),
        lax.all_gather(value_bias, ("wide", "narrow"), axis=0, tiled=True),
        lax.all_gather(out_weight, ("wide", "narrow"), axis=0, tiled=True),
        lax.all_gather(out_bias, ("wide", "narrow"), axis=0, tiled=True),
        lax.all_gather(second_gain, ("wide", "narrow"), axis=0, tiled=True),
        lax.all_gather(second_shift, ("wide", "narrow"), axis=0, tiled=True),
        lax.all_gather(up_weight, ("wide", "narrow"), axis=0, tiled=True),
        lax.all_gather(up_bias, ("wide", "narrow"), axis=0, tiled=True),
        lax.all_gather(down_weight, ("wide", "narrow"), axis=0, tiled=True),
        lax.all_gather(down_bias, ("wide", "narrow"), axis=0, tiled=True),
    )


def spread(parts):
    (
        first_gain,
        first_shift,
        query_weight,
        query_bias,
        key_weight,
        value_weight,
        value_bias,
        out_weight,
        out_bias,
        second_gain,
        second_shift,
        up_weight,
        up_bias,
        down_weight,
        down_bias,
    ) = parts
    return (
        lax.psum_scatter(first_gain, ("wide", "narrow"), scatter_dimension=0, tiled=True),
        lax.psum_scatter(first_shift, ("wide", "narrow"), scatter_dimension=0, tiled=True),
        lax.psum_scatter(query_weight, ("wide", "narrow"), scatter_dimension=0, tiled=True),
        lax.psum_scatter(query_bias, ("wide", "narrow"), scatter_dimension=0, tiled=True),
        lax.psum_scatter(key_weight, ("wide", "narrow"), scatter_dimension=0, tiled=True),
        lax.psum_scatter(value_weight, ("wide", "narrow"), scatter_dimension=0, tiled=True),
        lax.psum_scatter(value_bias, ("wide", "narrow"), scatter_dimension=0, tiled=True),
        lax.psum_scatter(out_weight, ("wide", "narrow"), scatter_dimension=0, tiled=True),
        lax.psum_scatter(out_bias, ("wide", "narrow"), scatter_dimension=0, tiled=True),
        lax.psum_scatter(second_gain, ("wide", "narrow"), scatter_dimension=0, tiled=True),
        lax.psum_scatter(second_shift, ("wide", "narrow"), scatter_dimension=0, tiled=True),
        lax.psum_scatter(up_weight, ("wide", "narrow"), scatter_dimension=0, tiled=True),
        lax.psum_scatter(up_bias, ("wide", "narrow"), scatter_dimension=0, tiled=True),
        lax.psum_scatter(down_weight, ("wide", "narrow"), scatter_dimension=0, tiled=True),
        lax.psum_scatter(down_bias, ("wide", "narrow"), scatter_dimension=0, tiled=True),
    )


def norm_forward(value, gain, shift):
    center = value - jnp.mean(value, -1, keepdims=True)
    inverse = lax.rsqrt(jnp.mean(center * center, -1, keepdims=True) + EPSILON)
    normed = center * inverse
    return (normed * gain.astype(jnp.float32) + shift.astype(jnp.float32), normed, inverse)


def norm_backward(incoming, normed, inverse, gain):
    scaled = incoming * gain.astype(jnp.float32)
    inner = (
        scaled
        - jnp.mean(scaled, -1, keepdims=True)
        - normed * jnp.mean(scaled * normed, -1, keepdims=True)
    )
    return (inverse * inner, jnp.sum(incoming * normed, 0), jnp.sum(incoming, 0))


def gelu_parts(hidden):
    cdf = 0.5 * (1.0 + lax.erf(hidden * 0.7071067811865476))
    density = jnp.exp(-0.5 * hidden * hidden) * 0.3989422804014327
    return (hidden * cdf, cdf + hidden * density)


def masked_scores(queries, keys, length):
    count = queries.shape[0]
    raw = jnp.einsum("qhd,khd->hqk", queries, keys, preferred_element_type=jnp.float32) * HD ** (
        -0.5
    )
    position = jnp.arange(count, dtype=jnp.int32)
    distance = (position[:, None] - position[None, :]).astype(jnp.float32)
    slopes = jnp.exp2(-8.0 * jnp.arange(1, H + 1, dtype=jnp.float32) / H)
    raw = raw - slopes[:, None, None] * distance[None]
    allowed = (position[:, None] >= position[None, :]) & (
        position[:, None] // length == position[None, :] // length
    )
    return jnp.where(allowed[None], raw, -1e30)


def forward(tokens, length, weights):
    (
        first_gain,
        first_shift,
        query_weight,
        query_bias,
        key_weight,
        value_weight,
        value_bias,
        out_weight,
        out_bias,
        second_gain,
        second_shift,
        up_weight,
        up_bias,
        down_weight,
        down_bias,
    ) = weights
    count = tokens.shape[0]
    width = tokens.shape[1]
    inputs = tokens.astype(jnp.float32)
    first_out, first_normed, first_inverse = norm_forward(inputs, first_gain, first_shift)
    attn_in = first_out.astype(jnp.bfloat16)
    queries = (
        (
            jnp.dot(attn_in, query_weight, preferred_element_type=jnp.float32)
            + query_bias.astype(jnp.float32)
        )
        .astype(jnp.bfloat16)
        .reshape(count, H, HD)
    )
    keys = (
        jnp.dot(attn_in, key_weight, preferred_element_type=jnp.float32)
        .astype(jnp.bfloat16)
        .reshape(count, H, HD)
    )
    values = (
        (
            jnp.dot(attn_in, value_weight, preferred_element_type=jnp.float32)
            + value_bias.astype(jnp.float32)
        )
        .astype(jnp.bfloat16)
        .reshape(count, H, HD)
    )
    scores = masked_scores(queries, keys, length)
    top = jnp.max(scores, -1, keepdims=True)
    expo = jnp.exp(scores - top)
    total = jnp.sum(expo, -1, keepdims=True)
    probs = expo / total
    log_total = top + jnp.log(total)
    mixed = jnp.einsum(
        "hqk,khd->qhd", probs.astype(jnp.bfloat16), values, preferred_element_type=jnp.float32
    )
    mixed = mixed.reshape(count, width).astype(jnp.bfloat16)
    resid = (
        inputs
        + jnp.dot(mixed, out_weight, preferred_element_type=jnp.float32)
        + out_bias.astype(jnp.float32)
    )
    second_out, second_normed, second_inverse = norm_forward(resid, second_gain, second_shift)
    ffn_in = second_out.astype(jnp.bfloat16)
    hidden = jnp.dot(ffn_in, up_weight, preferred_element_type=jnp.float32) + up_bias.astype(
        jnp.float32
    )
    active, active_slope = gelu_parts(hidden)
    active_low = active.astype(jnp.bfloat16)
    result = (
        resid
        + jnp.dot(active_low, down_weight, preferred_element_type=jnp.float32)
        + down_bias.astype(jnp.float32)
    )
    return (
        result.astype(jnp.bfloat16),
        attn_in,
        first_normed,
        first_inverse,
        queries,
        keys,
        values,
        log_total,
        mixed,
        second_normed,
        second_inverse,
        ffn_in,
        active_slope,
        active_low,
    )


def backward(cotangent, length, weights, kept):
    (
        first_gain,
        first_shift,
        query_weight,
        query_bias,
        key_weight,
        value_weight,
        value_bias,
        out_weight,
        out_bias,
        second_gain,
        second_shift,
        up_weight,
        up_bias,
        down_weight,
        down_bias,
    ) = weights
    (
        result,
        attn_in,
        first_normed,
        first_inverse,
        queries,
        keys,
        values,
        log_total,
        mixed,
        second_normed,
        second_inverse,
        ffn_in,
        active_slope,
        active_low,
    ) = kept
    count = cotangent.shape[0]
    width = cotangent.shape[1]
    grad_out = cotangent.astype(jnp.float32)
    grad_down_bias = jnp.sum(grad_out, 0)
    grad_down_weight = jnp.einsum(
        "tf,td->fd", active_low, cotangent, preferred_element_type=jnp.float32
    )
    grad_active = jnp.einsum(
        "td,fd->tf", cotangent, down_weight, preferred_element_type=jnp.float32
    )
    grad_hidden = (grad_active * active_slope).astype(jnp.bfloat16)
    grad_up_bias = jnp.sum(grad_hidden.astype(jnp.float32), 0)
    grad_up_weight = jnp.einsum(
        "td,tf->df", ffn_in, grad_hidden, preferred_element_type=jnp.float32
    )
    grad_ffn_in = jnp.einsum(
        "tf,df->td", grad_hidden, up_weight, preferred_element_type=jnp.float32
    )
    grad_second, grad_second_gain, grad_second_shift = norm_backward(
        grad_ffn_in, second_normed, second_inverse, second_gain
    )
    grad_resid = grad_out + grad_second
    grad_branch = grad_resid.astype(jnp.bfloat16)
    grad_out_bias = jnp.sum(grad_branch.astype(jnp.float32), 0)
    grad_out_weight = jnp.einsum(
        "tc,td->cd", mixed, grad_branch, preferred_element_type=jnp.float32
    )
    grad_mixed = jnp.einsum(
        "td,cd->tc", grad_branch, out_weight, preferred_element_type=jnp.float32
    )
    grad_mixed = grad_mixed.astype(jnp.bfloat16).reshape(count, H, HD)
    scores = masked_scores(queries, keys, length)
    probs = jnp.exp(scores - log_total)
    grad_probs = jnp.einsum("qhd,khd->hqk", grad_mixed, values, preferred_element_type=jnp.float32)
    grad_values = jnp.einsum(
        "hqk,qhd->khd", probs.astype(jnp.bfloat16), grad_mixed, preferred_element_type=jnp.float32
    )
    grad_values = grad_values.astype(jnp.bfloat16).reshape(count, width)
    row_total = jnp.sum(grad_probs * probs, -1, keepdims=True)
    grad_scores = (probs * (grad_probs - row_total)).astype(jnp.bfloat16)
    factor = HD ** (-0.5)
    grad_queries = (
        jnp.einsum("hqk,khd->qhd", grad_scores, keys, preferred_element_type=jnp.float32) * factor
    )
    grad_queries = grad_queries.astype(jnp.bfloat16).reshape(count, width)
    grad_keys = (
        jnp.einsum("hqk,qhd->khd", grad_scores, queries, preferred_element_type=jnp.float32)
        * factor
    )
    grad_keys = grad_keys.astype(jnp.bfloat16).reshape(count, width)
    grad_query_bias = jnp.sum(grad_queries.astype(jnp.float32), 0)
    grad_value_bias = jnp.sum(grad_values.astype(jnp.float32), 0)
    grad_query_weight = jnp.einsum(
        "tc,td->cd", attn_in, grad_queries, preferred_element_type=jnp.float32
    )
    grad_key_weight = jnp.einsum(
        "tc,td->cd", attn_in, grad_keys, preferred_element_type=jnp.float32
    )
    grad_value_weight = jnp.einsum(
        "tc,td->cd", attn_in, grad_values, preferred_element_type=jnp.float32
    )
    grad_attn = jnp.einsum(
        "td,cd->tc", grad_queries, query_weight, preferred_element_type=jnp.float32
    )
    grad_attn = grad_attn + jnp.einsum(
        "td,cd->tc", grad_keys, key_weight, preferred_element_type=jnp.float32
    )
    grad_attn = grad_attn + jnp.einsum(
        "td,cd->tc", grad_values, value_weight, preferred_element_type=jnp.float32
    )
    grad_first, grad_first_gain, grad_first_shift = norm_backward(
        grad_attn, first_normed, first_inverse, first_gain
    )
    grad_tokens = (grad_resid + grad_first).astype(jnp.bfloat16)
    sums = spread(
        (
            grad_first_gain,
            grad_first_shift,
            grad_query_weight,
            grad_query_bias,
            grad_key_weight,
            grad_value_weight,
            grad_value_bias,
            grad_out_weight,
            grad_out_bias,
            grad_second_gain,
            grad_second_shift,
            grad_up_weight,
            grad_up_bias,
            grad_down_weight,
            grad_down_bias,
        )
    )
    return (grad_tokens, sums)


def body(
    tokens,
    cotangent,
    seq_length,
    first_gain,
    first_shift,
    query_weight,
    query_bias,
    key_weight,
    value_weight,
    value_bias,
    out_weight,
    out_bias,
    second_gain,
    second_shift,
    up_weight,
    up_bias,
    down_weight,
    down_bias,
):
    shards = (
        first_gain,
        first_shift,
        query_weight,
        query_bias,
        key_weight,
        value_weight,
        value_bias,
        out_weight,
        out_bias,
        second_gain,
        second_shift,
        up_weight,
        up_bias,
        down_weight,
        down_bias,
    )
    length = seq_length[0]
    weights = collect(shards)
    kept = forward(tokens, length, weights)
    back_weights = collect(shards)
    grad_tokens, sums = backward(cotangent, length, back_weights, kept)
    (
        g_first_gain,
        g_first_shift,
        g_query_weight,
        g_query_bias,
        g_key_weight,
        g_value_weight,
        g_value_bias,
        g_out_weight,
        g_out_bias,
        g_second_gain,
        g_second_shift,
        g_up_weight,
        g_up_bias,
        g_down_weight,
        g_down_bias,
    ) = sums
    return (
        kept[0],
        grad_tokens,
        g_first_gain,
        g_first_shift,
        g_query_weight,
        g_query_bias,
        g_key_weight,
        g_value_weight,
        g_value_bias,
        g_out_weight,
        g_out_bias,
        g_second_gain,
        g_second_shift,
        g_up_weight,
        g_up_bias,
        g_down_weight,
        g_down_bias,
    )


def solution(mesh):
    placed = (
        P(("wide", "narrow"), None),
        P(("wide", "narrow"), None),
        P(("wide", "narrow")),
        P(("wide", "narrow")),
        P(("wide", "narrow")),
        P(("wide", "narrow"), None),
        P(("wide", "narrow")),
        P(("wide", "narrow"), None),
        P(("wide", "narrow"), None),
        P(("wide", "narrow")),
        P(("wide", "narrow"), None),
        P(("wide", "narrow")),
        P(("wide", "narrow")),
        P(("wide", "narrow")),
        P(("wide", "narrow"), None),
        P(("wide", "narrow")),
        P(("wide", "narrow"), None),
        P(("wide", "narrow")),
    )
    return jax.shard_map(
        body,
        mesh=mesh,
        in_specs=placed,
        out_specs=(
            P(("wide", "narrow"), None),
            P(("wide", "narrow"), None),
            P(("wide", "narrow")),
            P(("wide", "narrow")),
            P(("wide", "narrow"), None),
            P(("wide", "narrow")),
            P(("wide", "narrow"), None),
            P(("wide", "narrow"), None),
            P(("wide", "narrow")),
            P(("wide", "narrow"), None),
            P(("wide", "narrow")),
            P(("wide", "narrow")),
            P(("wide", "narrow")),
            P(("wide", "narrow"), None),
            P(("wide", "narrow")),
            P(("wide", "narrow"), None),
            P(("wide", "narrow")),
        ),
        check_vma=False,
    )
```

profile of v0, /device:TPU:2, one launch (start us, length us, event | category | flops | bytes accessed | tf_op | source)
XLA Modules:
  0.0 1389.1 jit_solution(1803479733588926766)
XLA Ops:
  11.3 2.7 subtract_convert_fusion
  16.5 41.7 %all-reduce.18 = (bf16[1024]{0:T(1024)(128)(2,1)S(1)}, bf16[1024]{0:T(1024)(128)(2,1)S(1)}, bf16[1024]{0:T(1024)(128)(2,1)S(1)}, bf16[1024]{0:T(1024)(128)(2,1)S...) all-reduce(bf16[1024]{0:T(1024)(128)(2,1)S(1)} %dynamic-update-slic, ...), channel_id=1, replica_groups=mesh['wide'=8,'narrow'=4] {'wide','narrow'}, use_global_device_ids=true, to_apply=%add.4 | all-reduce | flops 8192 | bytes 32768
  58.3 36.2 %all-gather = bf16[32,1,128]{2,1,0:T(2,128)(2,1)S(1)} all-gather(bf16[1,1,128]{2,1,0:T(2,128)(2,1)S(1)} %bitcast.79), channel_id=1, replica_groups=mesh['wide'=8,'narrow'=4] {'wide','narrow'}, dimensions={0}, use_global_device_ids=true | all-gather | bytes 8448 | tf_op jit(solution)/shard_map/all_gather | solution.py:44
  95.3 2.9 copy.53
  99.2 4.0 copy.58
  103.1 5.6 convolution_convert_fusion.1
  108.7 18.2 %all-gather.10.cloned.1.call-done = bf16[1024,1024]{1,0:T(8,128)(2,1)} async-done(((bf16[32,1024]{1,0:T(8,128)(2,1)}), bf16[1024,1024]{1,0:T(8,128)(2,1)}) %all-gather.10.cloned.1.call-update) | async-done | bytes 2097168 | tf_op jit(solution)/shard_map/all_gather | solution.py:34
  126.9 5.6 add_convert_fusion.2
  132.5 52.5 %all-gather.8.cloned.1.call-done = bf16[1024,1024]{1,0:T(8,128)(2,1)} async-done(((bf16[32,1024]{1,0:T(8,128)(2,1)}), bf16[1024,1024]{1,0:T(8,128)(2,1)}) %all-gather.8.cloned.1.call-update) | async-done | bytes 2097168 | tf_op jit(solution)/shard_map/all_gather | solution.py:37
  185.1 5.6 add_convert_fusion.3
  190.7 18.9 %fusion.48 = (f32[8,1024]{1,0:T(8,128)S(1)}, f32[8,1024,1024]{1,2,0:T(8,128)}) fusion(f32[1024,1024]{0,1:T(8,128)} %subtract_convert_fusion, f32[8]{0:T(128)S(1)} %multiply_exponential_fusion, bf16[1024,8,128]{0,2,1:T(8,128)(2,1)} %bitcast.63, bf16[1024,8,128]{0,2,1:T(8,128)(2,1)} %bitcast.71, pred[1024,1024]{0,1:T(8,128)(4,1)S(1)} %fusion.28), kind=kOutput, calls=%fused_computation.87 | convolution fusion | flops 2189418496 | bytes 43024416 | tf_op jit(solution)/shard_map/qhd,khd->hqk/dot_general | solution.py:112
  209.6 13.1 fusion
  222.7 15.8 %fusion.32 = bf16[8,128,1024]{2,1,0:T(8,128)(2,1)} fusion(bf16[1024,8,128]{0,2,1:T(8,128)(2,1)} %bitcast.69, f32[8,1024,1024]{1,2,0:T(8,128)} %get-tuple-element.79, f32[8,1024]{1,0:T(8,128)S(1)} %fusion, f32[8,1024]{1,0:T(8,128)S(1)} %get-tuple-element.78), kind=kOutput, calls=%fused_computation.64 | convolution fusion | flops 2173698048 | bytes 37814272 | tf_op jit(solution)/shard_map/hqk,khd->qhd/dot_general | solution.py:175
  238.6 4.5 all-gather.14.cloned.1.call-done
  243.1 5.0 fusion.49
  250.5 71.7 %all-gather.16.cloned.1.call-done = bf16[1024,4096]{1,0:T(8,128)(2,1)} async-done(((bf16[32,4096]{1,0:T(8,128)(2,1)}), bf16[1024,4096]{1,0:T(8,128)(2,1)}) %all-gather.16.cloned.1.call-update) | async-done | bytes 8388624 | tf_op jit(solution)/shard_map/all_gather | solution.py:43
  322.2 20.3 %multiply_convert_fusion.1 = (bf16[1024,4096]{1,0:T(8,128)(2,1)}, f32[1024,4096]{1,0:T(8,128)}) fusion(f32[4096]{0:T(1024)S(1)} %bitcast.76, bf16[1024,4096]{1,0:T(8,128)(2,1)} %all-gather.16.cloned.1.call-done, f32[1024,1024]{0,1:T(8,128)} %copy-done, f32[1024]{0:T(1024)S(1)} %convert_element_type.142, f32[1024]{0:T(1024)S(1)} %convert_element_type.141, ...), kind=kOutput, calls=%fused_computation.18 | convolution fusion | flops 8620343296 | bytes 37781504 | tf_op jit(solution)/shard_map/dot_general | solution.py:186
  342.5 58.6 %all-gather.18.cloned.1.call-done = bf16[4096,1024]{1,0:T(8,128)(2,1)} async-done(((bf16[128,1024]{1,0:T(8,128)(2,1)}), bf16[4096,1024]{1,0:T(8,128)(2,1)}) %all-gather.18.cloned.1.call-update) | async-done | bytes 8388624 | tf_op jit(solution)/shard_map/all_gather | solution.py:45
  401.1 18.8 %convert_reduce_fusion = (f32[4096]{0:T(1024)}, bf16[1024,4096]{1,0:T(8,128)(2,1)S(1)}) fusion(f32[1024,4096]{1,0:T(8,128)} %get-tuple-element.83, f32[4096]{0:T(1024)S(1)} %bitcast.77, bf16[1024,1024]{1,0:T(8,128)(2,1)} %param.19, bf16[4096,1024]{1,0:T(8,128)(2,1)} %all-gather.18.cloned.1.call-done), kind=kOutput, calls=%fused_computation.16 | convolution fusion | flops 8644456448 | bytes 35684352 | tf_op jit(solution)/shard_map/td,fd->tf/dot_general | solution.py:255
  419.9 11.2 fusion.50
  431.1 5.4 copy.59
  436.5 5.1 multiply_reduce_fusion.1
  442.5 4.7 convert_reduce_fusion.3
  449.2 4.3 fusion.34
  453.6 6.5 convolution_convert_fusion
  460.1 16.8 %convert_reduce_fusion.4 = (f32[8,128]{1,0:T(8,128)}, bf16[8,128,1024]{2,1,0:T(8,128)(2,1)}) fusion(bf16[1024,8,128]{0,2,1:T(8,128)(2,1)} %bitcast.61, f32[8,1024,1024]{1,2,0:T(8,128)} %get-tuple-element.79, f32[8,1024]{1,0:T(8,128)S(1)} %log_add_fusion), kind=kOutput, calls=%fused_computation.44 | convolution fusion | flops 2167405568 | bytes 37785600 | tf_op jit(solution)/shard_map/hqk,qhd->khd/dot_general | solution.py:282
  476.9 6.0 fusion.39
  483.0 23.1 %multiply_reduce_fusion = (f32[8,1024]{1,0:T(8,128)S(1)}, f32[8,1024,1024]{1,2,0:T(8,128)}) fusion(f32[8,1024,1024]{1,2,0:T(8,128)} %get-tuple-element.79, f32[8,1024]{1,0:T(8,128)S(1)} %log_add_fusion, bf16[1024,8,128]{0,2,1:T(8,128)(2,1)} %bitcast.62, bf16[1024,8,128]{0,2,1:T(8,128)(2,1)} %bitcast.70), kind=kOutput, calls=%fused_computation.1 | convolution fusion | flops 2172641280 | bytes 71368704 | tf_op jit(solution)/shard_map/qhd,khd->hqk/dot_general | solution.py:281
  506.1 28.4 %multiply_convert_fusion = bf16[8,1024,1024]{1,2,0:T(8,128)(2,1)} fusion(f32[8,1024,1024]{1,2,0:T(8,128)} %get-tuple-element.85, f32[8,1024,1024]{1,2,0:T(8,128)} %get-tuple-element.79, f32[8,1024]{1,0:T(8,128)S(1)} %get-tuple-element.84, f32[8,1024]{1,0:T(8,128)S(1)} %log_add_fusion), kind=kLoop, calls=%fused_computation | loop fusion | flops 33554432 | bytes 83951616 | tf_op jit(solution)/shard_map/convert_element_type | solution.py:287
  534.5 8.9 convert_reduce_fusion.5
  544.7 4.5 fusion.43
  549.5 13.5 multiply_convert_fusion.2
  563.0 5.9 fusion.41
  569.6 16.6 %fusion.37 = f32[1024,4096]{1,0:T(8,128)} fusion(bf16[1024,4096]{1,0:T(8,128)(2,1)} %copy-done.37, f32[1024,1024]{0,1:T(8,128)} %copy-done, f32[1024]{0:T(1024)S(1)} %copy-done.20, f32[1024]{0:T(1024)S(1)} %convert_element_type.141, f32[1024]{0:T(1024)S(1)} %add_rsqrt_fusion, f32[1024]{0:T(1024)S(1)} %broadcast_multiply_fusion.4), kind=kOutput, calls=%fused_computation.82 | convolution fusion | flops 8595177472 | bytes 29376512 | tf_op jit(solution)/shard_map/td,tf->df/dot_general | solution.py:260
  586.5 16.2 %fusion.51 = f32[4096,1024]{1,0:T(8,128)} fusion(bf16[1024,4096]{1,0:T(8,128)(2,1)} %get-tuple-element.82, bf16[1024,1024]{1,0:T(8,128)(2,1)} %param.19), kind=kOutput, calls=%fused_computation.90 | convolution fusion | flops 8589934592 | bytes 27262976 | tf_op jit(solution)/shard_map/tf,td->fd/dot_general | solution.py:252
  603.4 15.4 %add_convert_fusion = bf16[1024,1024]{0,1:T(8,128)(2,1)} fusion(f32[1024,1024]{0,1:T(8,128)} %copy-done, f32[1024]{0:T(1024)S(1)} %convert_element_type.146, bf16[1024,4096]{1,0:T(8,128)(2,1)} %get-tuple-element.82, bf16[4096,1024]{1,0:T(8,128)(2,1)} %all-gather.18.cloned.1.call-done), kind=kOutput, calls=%fused_computation.50 | convolution fusion | flops 8593080320 | bytes 23072768 | tf_op jit(solution)/shard_map/dot_general | solution.py:193
  618.8 4.2 copy.69
  623.0 4.7 fusion.52
  627.7 2.3 fusion.53
  630.2 5.2 fusion.25
  635.4 41.7 %all-reduce.17 = (f32[1024]{0:T(1024)S(1)}, f32[1024]{0:T(1024)S(1)}, f32[1024]{0:T(1024)S(1)}, f32[1024]{0:T(1024)S(1)}, f32[1024]{0:T(1024)S(1)}, /*index=5*/f...) all-reduce(f32[1024]{0:T(1024)S(1)} %get-tuple-element.53, ...), channel_id=2, replica_groups=mesh['wide'=8,'narrow'=4] {'wide','narrow'}, use_global_device_ids=true, to_apply=%region_12.13.clone | all-reduce | flops 12288 | bytes 98304
  681.8 6.2 fusion.24
  688.0 3.9 copy.70
  692.5 31.4 %reduce-scatter.11.cloned.1.call-done = f32[32,1024]{1,0:T(8,128)} async-done(((f32[1024,1024]{1,0:T(8,128)}), f32[32,1024]{1,0:T(8,128)}) %reduce-scatter.11.cloned.1.call-update) | async-done | bytes 131088 | tf_op jit(solution)/shard_map/reduce_scatter | solution.py:74
  723.9 140.1 %reduce-scatter.7.cloned.1.call-done = f32[32,1024]{1,0:T(8,128)} async-done(((f32[1024,1024]{1,0:T(8,128)}), f32[32,1024]{1,0:T(8,128)}) %reduce-scatter.7.cloned.1.call-update) | async-done | bytes 131088 | tf_op jit(solution)/shard_map/reduce_scatter | solution.py:71
  863.9 140.2 %reduce-scatter.9.cloned.1.call-done = f32[32,1024]{1,0:T(8,128)} async-done(((f32[1024,1024]{1,0:T(8,128)}), f32[32,1024]{1,0:T(8,128)}) %reduce-scatter.9.cloned.1.call-update) | async-done | bytes 131088 | tf_op jit(solution)/shard_map/reduce_scatter | solution.py:73
  1004.1 190.2 %reduce-scatter.15.cloned.1.call-done = f32[32,4096]{1,0:T(8,128)} async-done(((f32[1024,4096]{1,0:T(8,128)}), f32[32,4096]{1,0:T(8,128)}) %reduce-scatter.15.cloned.1.call-update) | async-done | bytes 524304 | tf_op jit(solution)/shard_map/reduce_scatter | solution.py:80
  1194.3 187.7 %reduce-scatter.17.cloned.1.call-done = f32[128,1024]{1,0:T(8,128)} async-done(((f32[4096,1024]{1,0:T(8,128)}), f32[128,1024]{1,0:T(8,128)}) %reduce-scatter.17.cloned.1.call-update) | async-done | bytes 524304 | tf_op jit(solution)/shard_map/reduce_scatter | solution.py:82
  (150 shorter events, 21.3 us)
Async XLA Ops:
  7.2 7.4 copy-start.28
  7.2 7.7 copy-start.29
  7.2 7.9 copy-start.30
  7.2 8.1 copy-start.31
  7.2 8.4 copy-start.32
  7.2 8.6 copy-start.33
  7.3 8.8 copy-start.34
  7.3 9.0 copy-start.35
  7.3 51.1 %copy-start.24 = (bf16[128]{0:T(256)(128)(2,1)S(1)}, bf16[128]{0:T(256)(128)(2,1)}, u32[]{:S(2)}) copy-start(bf16[128]{0:T(256)(128)(2,1)} %param.33) | copy-start | bytes 772
  7.3 95.8 %all-gather.12.cloned.1.call-start = ((), (), s32[]{:S(2)}) async-start(), calls=%async_computation.8 | async-start | bytes 2162688 | tf_op jit(solution)/shard_map/all_gather | solution.py:36
  8.0 118.9 %all-gather.10.cloned.1.call-start = ((), (), s32[]{:S(2)}) async-start(), calls=%async_computation.7 | async-start | bytes 2162688 | tf_op jit(solution)/shard_map/all_gather | solution.py:34
  8.8 176.3 %all-gather.8.cloned.1.call-start = ((), (), s32[]{:S(2)}) async-start(), calls=%async_computation.6 | async-start | bytes 2162688 | tf_op jit(solution)/shard_map/all_gather | solution.py:37
  9.5 233.6 %all-gather.14.cloned.1.call-start = ((), (), s32[]{:S(2)}) async-start(), calls=%async_computation.9 | async-start | bytes 2162688 | tf_op jit(solution)/shard_map/all_gather | solution.py:39
  10.1 312.1 %all-gather.16.cloned.1.call-start = ((), (), s32[]{:S(2)}) async-start(), calls=%async_computation.10 | async-start | bytes 8650752 | tf_op jit(solution)/shard_map/all_gather | solution.py:43
  10.7 390.5 %all-gather.18.cloned.1.call-start = ((), (), s32[]{:S(2)}) async-start(), calls=%async_computation.11 | async-start | bytes 8650752 | tf_op jit(solution)/shard_map/all_gather | solution.py:45
  11.2 681.2 %reduce-scatter.13.cloned.1.call-start = ((), (), s32[]{:S(2)}) async-start(), calls=%async_computation.15 | async-start | bytes 4325376 | tf_op jit(solution)/shard_map/reduce_scatter | solution.py:76
  58.2 126.8 %copy-start.13 = (f32[1024]{0:T(1024)}, f32[1024]{0:T(1024)S(1)}, u32[]{:S(2)}) copy-start(f32[1024]{0:T(1024)S(1)} %convert_element_type.127) | copy-start | bytes 12292
  58.3 126.8 %copy-start.21 = (f32[1024]{0:T(1024)}, f32[1024]{0:T(1024)S(1)}, u32[]{:S(2)}) copy-start(f32[1024]{0:T(1024)S(1)} %convert_element_type.128) | copy-start | bytes 12292
  58.3 263.9 %copy-start.19 = (f32[1024]{0:T(1024)}, f32[1024]{0:T(1024)S(1)}, u32[]{:S(2)}) copy-start(f32[1024]{0:T(1024)S(1)} %convert_element_type.142) | copy-start | bytes 12292
  98.5 86.5 %copy-start.7 = (f32[1024]{0:T(1024)}, f32[1024]{0:T(1024)S(1)}, u32[]{:S(2)}) copy-start(f32[1024]{0:T(1024)S(1)} %broadcast_multiply_fusion.5) | copy-start | bytes 12292
  99.1 85.9 %copy-start.15 = (f32[1024]{0:T(1024)}, f32[1024]{0:T(1024)S(1)}, u32[]{:S(2)}) copy-start(f32[1024]{0:T(1024)S(1)} %add_rsqrt_fusion.1) | copy-start | bytes 12292
  248.1 1.9 copy-start
  401.1 18.8 %copy-start.25 = (bf16[1024,4096]{1,0:T(8,128)(2,1)S(1)}, bf16[1024,4096]{1,0:T(8,128)(2,1)}, u32[]{:S(2)}) copy-start(bf16[1024,4096]{1,0:T(8,128)(2,1)} %all-gather.16.cloned.1.call-done) | copy-start | bytes 25165828
  419.9 11.2 copy-start.37
  436.5 5.1 copy-start.1
  436.5 5.9 copy-start.2
  442.5 6.7 copy-start.36
  447.2 2.0 copy-start.3
  453.5 270.4 %reduce-scatter.11.cloned.1.call-start = ((), (), s32[]{:S(2)}) async-start(), calls=%async_computation.14 | async-start | bytes 4325376 | tf_op jit(solution)/shard_map/reduce_scatter | solution.py:74
  460.1 16.8 %copy-start.8 = (f32[1024]{0:T(1024)S(1)}, f32[1024]{0:T(1024)}, u32[]{:S(2)}) copy-start(f32[1024]{0:T(1024)} %copy-done.7) | copy-start | bytes 12292
  460.1 16.8 %copy-start.14 = (f32[1024]{0:T(1024)S(1)}, f32[1024]{0:T(1024)}, u32[]{:S(2)}) copy-start(f32[1024]{0:T(1024)} %copy-done.13) | copy-start | bytes 12292
  460.1 16.8 %copy-start.16 = (f32[1024]{0:T(1024)S(1)}, f32[1024]{0:T(1024)}, u32[]{:S(2)}) copy-start(f32[1024]{0:T(1024)} %copy-done.15) | copy-start | bytes 12292
  460.1 16.8 %copy-start.22 = (f32[1024]{0:T(1024)S(1)}, f32[1024]{0:T(1024)}, u32[]{:S(2)}) copy-start(f32[1024]{0:T(1024)} %copy-done.21) | copy-start | bytes 12292
  483.0 381.0 %reduce-scatter.7.cloned.1.call-start = ((), (), s32[]{:S(2)}) async-start(), calls=%async_computation.12 | async-start | bytes 4325376 | tf_op jit(solution)/shard_map/reduce_scatter | solution.py:71
  543.4 1.3 copy-start.6
  549.3 454.8 %reduce-scatter.9.cloned.1.call-start = ((), (), s32[]{:S(2)}) async-start(), calls=%async_computation.13 | async-start | bytes 4325376 | tf_op jit(solution)/shard_map/reduce_scatter | solution.py:73
  568.9 625.4 %reduce-scatter.15.cloned.1.call-start = ((), (), s32[]{:S(2)}) async-start(), calls=%async_computation.16 | async-start | bytes 17301504 | tf_op jit(solution)/shard_map/reduce_scatter | solution.py:80
  586.2 795.8 %reduce-scatter.17.cloned.1.call-start = ((), (), s32[]{:S(2)}) async-start(), calls=%async_computation.17 | async-start | bytes 17301504 | tf_op jit(solution)/shard_map/reduce_scatter | solution.py:82
  623.0 4.7 copy-start.4
  623.0 4.7 copy-start.26
  627.7 2.4 copy-start.5
  627.7 2.4 copy-start.27
  630.1 5.3 copy-start.9
  630.1 5.3 copy-start.10
  630.1 5.3 copy-start.11
  630.1 5.3 copy-start.12
  630.1 5.3 copy-start.17
  630.1 5.3 copy-start.18
  (2 other events, 1.4 us)
Sparse Core Ops, SparseCore 0:
  11.0 57.5 all-gather.11
  71.4 55.4 all-gather.9
  129.8 55.2 all-gather.7
  187.8 55.2 all-gather.13
  245.8 76.3 all-gather.15
  324.9 76.1 all-gather.17
  453.6 130.1 reduce-scatter.12
  586.6 137.1 reduce-scatter.10
  726.7 137.1 reduce-scatter.6
  866.6 137.4 reduce-scatter.8
  1007.0 187.2 reduce-scatter.14
  1197.0 184.8 reduce-scatter.16
where the time goes:
time: 1400 us; the launch traced here: 1390 us
  waiting for transfers between devices  899 us (64%)
  matrix products  257 us (18%)
  blocking collectives  120 us (9%)
  other arithmetic  62.5 us (4%)
  local copies, waits for them, and re-layouts  34.8 us (2%)
  between operations  15.6 us (1%)
    reduce_scatter x1, waiting for transfers between devices, spread(): lax.psum_scatter(up_weight, ('wide', 'narrow'), scatter_dimension=0, tile...  190 us
    reduce_scatter x1, waiting for transfers between devices, spread(): lax.psum_scatter(down_weight, ('wide', 'narrow'), scatter_dimension=0, ti...  188 us
    reduce_scatter x1, waiting for transfers between devices, spread(): lax.psum_scatter(key_weight, ('wide', 'narrow'), scatter_dimension=0, til...  140 us
    reduce_scatter x1, waiting for transfers between devices, spread(): lax.psum_scatter(query_weight, ('wide', 'narrow'), scatter_dimension=0, t...  140 us
    unnamed x2, blocking collectives  83.4 us
    all_gather x1, waiting for transfers between devices, collect(): lax.all_gather(up_weight, ('wide', 'narrow'), axis=0, tiled=True)  71.7 us
    all_gather x1, waiting for transfers between devices, collect(): lax.all_gather(down_weight, ('wide', 'narrow'), axis=0, tiled=True)  58.6 us
    all_gather x1, waiting for transfers between devices, collect(): lax.all_gather(value_weight, ('wide', 'narrow'), axis=0, tiled=True)  52.5 us
  transfers between devices with their start and end apart: 12, of which 10 were waited for; matrix products, arithmetic and copies ran while one was open for 21% of the time, Pallas kernels for 0%

commit v1 on v0

--- a/solution.py
+++ b/solution.py
@@ -1,16 +1,447 @@
+import functools
+
 import jax
 import jax.numpy as jnp
 from jax import lax
+from jax.experimental import pallas as pl
+from jax.experimental.pallas import tpu as pltpu
 from jax.sharding import PartitionSpec as P
 
 H = 8
 HD = 128
-
+AXES = ("wide", "narrow")
+MESH = pl.DeviceIdType.MESH
+BF = jnp.bfloat16
+F32 = jnp.float32
+
+
+class Place:
+    def __init__(self):
+        wide, narrow = lax.axis_index("wide"), lax.axis_index("narrow")
+        self.z, self.x = lax.div(wide, 2), lax.rem(wide, 2)
+        self.y, self.c = lax.div(narrow, 2), lax.rem(narrow, 2)
+        c, x, y = self.c, self.x, self.y
+        self.one = (x + (1 - c) * (1 - 2 * x), y + c * (1 - 2 * y))
+        self.two = (x + c * (1 - 2 * x), y + (1 - c) * (1 - 2 * y))
+        self.far = (1 - x, 1 - y)
+        self.here = (x, y)
+
+    def device(self, z, xy, c):
+        return (z * 2 + xy[0], xy[1] * 2 + c)
+
+    def up(self, step):
+        return lax.rem(self.z + step, 4)
+
+    def down(self, step):
+        return lax.rem(self.z + 4 - step, 4)
+
+    def partners(self):
+        z, c = self.z, self.c
+        return [self.device(self.up(step), self.here, c) for step in (1, 2, 3)] + [
+            self.device(z, self.one, c),
+            self.device(z, self.two, c),
+            self.device(z, self.here, 1 - c),
+        ]
+
+    def greet(self):
+        barrier = pltpu.get_barrier_semaphore()
+        partners = self.partners()
+        for partner in partners:
+            pl.semaphore_signal(barrier, inc=1, device_id=partner, device_id_type=MESH)
+        pl.semaphore_wait(barrier, len(partners))
+
+
+def remote(source, target, send, recv, device):
+    return pltpu.make_async_remote_copy(
+        src_ref=source,
+        dst_ref=target,
+        send_sem=send,
+        recv_sem=recv,
+        device_id=device,
+        device_id_type=MESH,
+    )
+
+
+class Gathering:
+    SEMS = 10
+    STAGES = 5
+
+    def __init__(self, place, local, full, send, recv, keep):
+        self.place, self.local, self.full = place, local, full
+        self.send, self.recv, self.keep = send, recv, keep
+
+    def block(self, xy, c):
+        return self.full.at[:, xy[0], xy[1], c]
+
+    def cell(self, z):
+        place = self.place
+        return self.full.at[z, place.x, place.y, place.c]
+
+    def copy(self, source, target, sem, device):
+        return remote(source, target, self.send.at[sem], self.recv.at[sem], device)
+
+    def along(self, step):
+        place = self.place
+        device = place.device(place.up(step), place.here, place.c)
+        return self.copy(self.local, self.cell(place.z), step - 1, device)
+
+    def pieces(self):
+        place = self.place
+        z, c = place.z, place.c
+        one, two = place.device(z, place.one, c), place.device(z, place.two, c)
+        twin = place.device(z, place.here, 1 - c)
+        mine, first = self.block(place.here, c), self.block(place.one, c)
+        second, far = self.block(place.two, c), self.block(place.far, c)
+        return {
+            3: (mine, one, self.block(place.one, c)),
+            4: (mine, two, self.block(place.two, c)),
+            5: (mine, twin, self.block(place.here, 1 - c)),
+            6: (first, two, self.block(place.far, c)),
+            7: (first, twin, self.block(place.two, 1 - c)),
+            8: (second, twin, self.block(place.one, 1 - c)),
+            9: (far, twin, self.block(place.far, 1 - c)),
+        }
+
+    def start(self, sem):
+        source, device, _ = self.pieces()[sem]
+        self.copy(source, source, sem, device).start()
+
+    def await_recv(self, sem):
+        _, device, landing = self.pieces()[sem]
+        self.copy(landing, landing, sem, device).wait_recv()
+
+    def own(self):
+        return pltpu.make_async_copy(self.local, self.cell(self.place.z), self.keep)
+
+    def stage(self, number):
+        place = self.place
+        if number == 0:
+            self.own().start()
+            for step in (1, 2, 3):
+                self.along(step).start()
+        elif number == 1:
+            self.own().wait()
+            for step in (1, 2, 3):
+                cell = self.cell(place.down(step))
+                device = place.device(place.down(step), place.here, place.c)
+                self.copy(cell, cell, step - 1, device).wait_recv()
+            for sem in (3, 4, 5):
+                self.start(sem)
+        elif number == 2:
+            self.await_recv(3)
+            self.start(6)
+            self.start(7)
+            self.await_recv(4)
+            self.start(8)
+        elif number == 3:
+            self.await_recv(6)
+            self.start(9)
+        elif number == 4:
+            for sem in (5, 7, 8, 9):
+                self.await_recv(sem)
+
+    def finish(self):
+        for step in (1, 2, 3):
+            self.along(step).wait_send()
+        for sem in range(3, 10):
+            source, device, _ = self.pieces()[sem]
+            self.copy(source, source, sem, device).wait_send()
+
+
+class Scattering:
+    SEMS = 7
+    STAGES = 5
+
+    def __init__(self, place, partial, mine, total, pair, line, out, send, recv, load):
+        self.place, self.partial, self.mine = place, partial, mine
+        self.total, self.pair, self.line, self.out = total, pair, line, out
+        self.send, self.recv, self.load = send, recv, load
+
+    def pieces(self):
+        place = self.place
+        z, c = place.z, place.c
+        one, two = place.device(z, place.one, c), place.device(z, place.two, c)
+        twin = place.device(z, place.here, 1 - c)
+        total = self.total
+
+        def block(xy):
+            return total.at[:, xy[0], xy[1]]
+
+        table = {
+            0: (self.partial.at[:, :, :, 1 - c], total, twin),
+            1: (block(place.two), self.pair.at[0], two),
+            2: (block(place.far), self.pair.at[1], two),
+            3: (block(place.one), self.pair.at[2], one),
+        }
+        for step in (1, 2, 3):
+            device = place.device(place.up(step), place.here, c)
+            table[3 + step] = (
+                total.at[place.up(step), place.x, place.y],
+                self.line.at[step - 1],
+                device,
+            )
+        return table
+
+    def copy(self, sem):
+        source, target, device = self.pieces()[sem]
+        return remote(source, target, self.send.at[sem], self.recv.at[sem], device)
+
+    def own(self):
+        return pltpu.make_async_copy(
+            self.partial.at[:, :, :, self.place.c], self.mine, self.load
+        )
+
+    def stage(self, number):
+        place, total, pair = self.place, self.total, self.pair
+
+        def add(xy, slot):
+            def body(z, carry):
+                value = total[z, xy[0], xy[1]].astype(F32) + pair[slot, z].astype(F32)
+                total[z, xy[0], xy[1]] = value.astype(BF)
+                return carry
+
+            lax.fori_loop(0, 4, body, 0)
+
+        if number == 0:
+            self.own().start()
+            self.copy(0).start()
+        elif number == 1:
+            self.own().wait()
+            self.copy(0).wait_recv()
+
+            def body(z, carry):
+                for x in range(2):
+                    for y in range(2):
+                        value = total[z, x, y].astype(F32) + self.mine[z, x, y].astype(F32)
+                        total[z, x, y] = value.astype(BF)
+                return carry
+
+            lax.fori_loop(0, 4, body, 0)
+            self.copy(2).start()
+            self.copy(1).start()
+        elif number == 2:
+            self.copy(2).wait_recv()
+            add(place.one, 1)
+            self.copy(3).start()
+            self.copy(1).wait_recv()
+            add(place.here, 0)
+        elif number == 3:
+            self.copy(3).wait_recv()
+            add(place.here, 2)
+            for step in (1, 2, 3):
+                self.copy(3 + step).start()
+        elif number == 4:
+            value = total[place.z, place.x, place.y].astype(F32)
+            for step in (1, 2, 3):
+                self.copy(3 + step).wait_recv()
+                value = value + self.line[step - 1].astype(F32)
+            self.out[...] = value
+
+    def finish(self):
+        for sem in range(7):
+            self.copy(sem).wait_send()
+
+
+class Summing:
+    SEMS = 6
+
+    def __init__(self, place, value, total, slots, send, recv):
+        self.place, self.value, self.total, self.slots = place, value, total, slots
+        self.send, self.recv = send, recv
+
+    def copy(self, sem):
+        place = self.place
+        device = [
+            place.device(place.z, place.here, 1 - place.c),
+            place.device(place.z, place.one, place.c),
+            place.device(place.z, place.two, place.c),
+        ] + [place.device(place.up(step), place.here, place.c) for step in (1, 2, 3)]
+        source = self.total.at[min(sem, 3)]
+        return remote(source, self.slots.at[sem], self.send.at[sem], self.recv.at[sem], device[sem])
+
+    def stage(self, number):
+        total, slots = self.total, self.slots
+        if number == 0:
+            total[0] = self.value[...]
+            self.copy(0).start()
+        elif number < 3:
+            self.copy(number - 1).wait_recv()
+            total[number] = total[number - 1] + slots[number - 1]
+            self.copy(number).start()
+        elif number == 3:
+            self.copy(2).wait_recv()
+            total[3] = total[2] + slots[2]
+            for sem in (3, 4, 5):
+                self.copy(sem).start()
+        elif number == 4:
+            value = total[3]
+            for sem in (3, 4, 5):
+                self.copy(sem).wait_recv()
+                value = value + slots[sem]
+            total[4] = value
+
+    def finish(self):
+        for sem in range(6):
+            self.copy(sem).wait_send()
+
+
+def pipeline(tasks, stages):
+    for tick in range(len(tasks) + stages - 1):
+        for number in reversed(range(stages)):
+            if 0 <= tick - number < len(tasks):
+                tasks[tick - number].stage(number)
+
+
+def halves(ref, count, width):
+    if count == 1:
+        return [ref]
+    lead = (slice(None),) * (len(ref.shape) - 1)
+    return [ref.at[lead + (pl.ds(i * width, width),)] for i in range(count)]
+
+
+CUTS = (1, 1, 1, 1, 1, 2, 2)
+
+
+def gather_kernel(*refs):
+    count = len(CUTS)
+    local, full = refs[:count], refs[count : 2 * count]
+    send, recv, keep = refs[2 * count :]
+    place = Place()
+    place.greet()
+    tasks = []
+    for source, target, cut in zip(local, full, CUTS):
+        width = source.shape[-1] // cut
+        for one, other in zip(halves(source, cut, width), halves(target, cut, width)):
+            g = len(tasks)
+            tasks.append(Gathering(place, one, other, send.at[g], recv.at[g], keep.at[g]))
+    pipeline(tasks, Gathering.STAGES)
+    for task in tasks:
+        task.finish()
+
+
+def gather_all(arrays):
+    groups = sum(CUTS)
+    results = pl.pallas_call(
+        gather_kernel,
+        out_shape=[jax.ShapeDtypeStruct((4, 2, 2, 2) + a.shape, a.dtype) for a in arrays],
+        in_specs=[pl.BlockSpec(memory_space=pltpu.HBM)] * len(arrays),
+        out_specs=[pl.BlockSpec(memory_space=pltpu.HBM)] * len(arrays),
+        scratch_shapes=[
+            pltpu.SemaphoreType.DMA((groups, Gathering.SEMS)),
+            pltpu.SemaphoreType.DMA((groups, Gathering.SEMS)),
+            pltpu.SemaphoreType.DMA((groups,)),
+        ],
+        compiler_params=pltpu.CompilerParams(collective_id=0, has_side_effects=True),
+    )(*arrays)
+    return results
+
+
+def scatter_kernel(cuts, *refs):
+    count = len(cuts)
+    small, partial = refs[0], refs[1 : 1 + count]
+    small_out, out = refs[1 + count], refs[2 + count : 2 + 2 * count]
+    rest = list(refs[2 + 2 * count :])
+    mine, total, pair, line = (rest[i * count : (i + 1) * count] for i in range(4))
+    small_total, small_slots, small_send, small_recv, send, recv, load = rest[4 * count :]
+    place = Place()
+    place.greet()
+    tasks = []
+    g = 0
+    for i, cut in enumerate(cuts):
+        width = partial[i].shape[-1] // cut
+        views = [
+            halves(ref, cut, width)
+            for ref in (partial[i], mine[i], total[i], pair[i], line[i], out[i])
+        ]
+        for j in range(cut):
+            tasks.append(
+                Scattering(place, *(view[j] for view in views), send.at[g], recv.at[g], load.at[g])
+            )
+            g += 1
+    sums = Summing(place, small, small_total, small_slots, small_send, small_recv)
+    tasks.insert(1, sums)
+    pipeline(tasks, Scattering.STAGES)
+    for task in tasks:
+        task.finish()
+    small_out[...] = small_total[4]
+
+
+def scatter_all(small, arrays, cuts):
+    groups = sum(cuts)
+    shards = [a.shape[4:] for a in arrays]
+    vmem = pl.BlockSpec(memory_space=pltpu.VMEM)
+    results = pl.pallas_call(
+        functools.partial(scatter_kernel, cuts),
+        out_shape=[jax.ShapeDtypeStruct(small.shape, F32)]
+        + [jax.ShapeDtypeStruct(s, F32) for s in shards],
+        in_specs=[vmem] + [pl.BlockSpec(memory_space=pltpu.HBM)] * len(arrays),
+        out_specs=[vmem] * (1 + len(arrays)),
+        scratch_shapes=[pltpu.VMEM((4, 2, 2) + s, BF) for s in shards]
+        + [pltpu.VMEM((4, 2, 2) + s, BF) for s in shards]
+        + [pltpu.VMEM((3, 4) + s, BF) for s in shards]
+        + [pltpu.VMEM((3,) + s, BF) for s in shards]
+        + [
+            pltpu.VMEM((5,) + small.shape, F32),
+            pltpu.VMEM((6,) + small.shape, F32),
+            pltpu.SemaphoreType.DMA((Summing.SEMS,)),
+            pltpu.SemaphoreType.DMA((Summing.SEMS,)),
+            pltpu.SemaphoreType.DMA((groups, Scattering.SEMS)),
+            pltpu.SemaphoreType.DMA((groups, Scattering.SEMS)),
+            pltpu.SemaphoreType.DMA((groups,)),
+        ],
+        compiler_params=pltpu.CompilerParams(
+            collective_id=1, has_side_effects=True, vmem_limit_bytes=60 << 20
+        ),
+    )(small, *arrays)
+    return results[0], results[1:]
+
+
+SMALL = (0, 1, 3, 6, 8, 9, 10, 14, 12)
+LARGE = (2, 4, 5, 7, 11, 13)
+
+
+def collect_fast(parts):
+    flat = jnp.concatenate([parts[i].astype(F32) for i in SMALL]).reshape(-1, 128)
+    flat = jnp.pad(flat, ((0, 8 - flat.shape[0]), (0, 0)))
+    small, *large = gather_all([flat] + [parts[i] for i in LARGE])
+    small = small.reshape(32, -1)
+    whole = [None] * len(parts)
+    start = 0
+    for i in SMALL:
+        size = parts[i].shape[0]
+        whole[i] = small[:, start : start + size].reshape(-1).astype(parts[i].dtype)
+        start += size
+    for i, array in zip(LARGE, large):
+        whole[i] = array.reshape(-1, array.shape[-1])
+    return tuple(whole)
+
+
+def spread_fast(parts):
+    small = jnp.concatenate([parts[i] for i in SMALL]).reshape(-1, 1024)
+    rows = small.shape[0]
+    small = jnp.pad(small, ((0, 16 - rows), (0, 0)))
+    order = (13, 11, 7, 2, 4, 5)
+    arrays = [
+        parts[i].astype(BF).reshape(4, 2, 2, 2, parts[i].shape[0] // 32, parts[i].shape[1])
+        for i in order
+    ]
+    small, large = scatter_all(small, arrays, (2, 2, 1, 1, 1, 1))
+    result = [None] * len(parts)
+    for i, array in zip(order, large):
+        result[i] = array
+    flat = small.reshape(-1)
+    me = lax.axis_index("wide") * 4 + lax.axis_index("narrow")
+    start = 0
+    for i in SMALL:
+        size = parts[i].shape[0]
+        result[i] = lax.dynamic_slice(flat, (start + me * (size // 32),), (size // 32,))
+        start += size
+    return tuple(result)
 
 EPSILON = 1e-05
 
 
-def collect(parts):
+def collect_plain(parts):
     (
         first_gain,
         first_shift,
@@ -47,7 +478,7 @@
     )
 
 
-def spread(parts):
+def spread_plain(parts):
     (
         first_gain,
         first_shift,
@@ -82,6 +513,18 @@
         lax.psum_scatter(down_weight, ("wide", "narrow"), scatter_dimension=0, tiled=True),
         lax.psum_scatter(down_bias, ("wide", "narrow"), scatter_dimension=0, tiled=True),
     )
+
+
+def is_fast():
+    return lax.axis_size("wide") == 8 and lax.axis_size("narrow") == 4
+
+
+def collect(parts):
+    return collect_fast(parts) if is_fast() else collect_plain(parts)
+
+
+def spread(parts):
+    return spread_fast(parts) if is_fast() else spread_plain(parts)
 
 
 def norm_forward(value, gain, shift):
@@ -381,8 +824,7 @@
     length = seq_length[0]
     weights = collect(shards)
     kept = forward(tokens, length, weights)
-    back_weights = collect(shards)
-    grad_tokens, sums = backward(cotangent, length, back_weights, kept)
+    grad_tokens, sums = backward(cotangent, length, weights, kept)
     (
         g_first_gain,
         g_first_shift,

time: 1400 us -> 622 us (0.44)
  waiting for transfers between devices: 899 us -> 0 us
  Pallas kernels: 0 us -> 269 us
  blocking collectives: 120 us -> 0 us
  matrix products: 257 us -> 243 us
    reduce_scatter x6 -> x0, waiting for transfers between devices: 689 us -> none  [the longest x1 190 us: spread(): lax.psum_scatter(up_weight, ('wide', 'narrow'), scatter_dimension=0, tile...]
    pallas_call x0 -> x2, Pallas kernels: none -> 269 us  [the longest x1 140 us: scatter_all(): pl.pallas_call(functools.partial(scatter_kernel, cuts), out_shape=[jax.Sh...]
    all_gather x6 -> x0, waiting for transfers between devices: 206 us -> none  [the longest x1 71.7 us: collect(): lax.all_gather(up_weight, ('wide', 'narrow'), axis=0, tiled=True)]
    unnamed x2 -> x0, blocking collectives: 83.4 us -> none
    all_gather x1 -> x0, blocking collectives: 36.2 us -> none  [collect(): lax.all_gather(up_bias, ('wide', 'narrow'), axis=0, tiled=True)]
    unnamed x105 -> x88, local copies, waits for them, and re-layouts: 29.4 us -> 26 us
  transfers between devices with their start and end apart: 12 -> 0, of which waited for: 10 -> 0; matrix products, arithmetic and copies ran while one was open for 21% -> 0% of each run, Pallas kernels for 0% -> 0%
where the time goes in v1:
time: 622 us; the launch traced here: 615 us
  Pallas kernels  269 us (43%)
  matrix products  243 us (39%)
  other arithmetic  60.7 us (10%)
  local copies, waits for them, and re-layouts  40.5 us (7%)
    pallas_call x1, Pallas kernels, scatter_all(): pl.pallas_call(functools.partial(scatter_kernel, cuts), out_shape=[jax.Sh...  140 us
    pallas_call x1, Pallas kernels, gather_all(): pl.pallas_call(gather_kernel, out_shape=[jax.ShapeDtypeStruct((4, 2, 2, 2...  129 us
    convert_element_type x1, other arithmetic, backward(): grad_scores = (probs * (grad_probs - row_total)).astype(jnp.bfloat16)  28.3 us
    unnamed x88, local copies, waits for them, and re-layouts  26 us
    dot_general x1, matrix products, backward(): jnp.einsum('qhd,khd->hqk', grad_mixed, values, preferred_element_type=jnp...  22.2 us
    dot_general x1, matrix products, forward(): jnp.dot(ffn_in, up_weight, preferred_element_type=jnp.float32)  20.2 us
    dot_general x1, matrix products, masked_scores(): jnp.einsum('qhd,khd->hqk', queries, keys, preferred_element_type=jnp.floa...  19.7 us
    dot_general x1, matrix products, backward(): jnp.einsum('td,fd->tf', cotangent, down_weight, preferred_element_type=jn...  19.3 us

profile of v1, /device:TPU:2, one launch (start us, length us, event | category | flops | bytes accessed | tf_op | source)
XLA Modules:
  0.0 615.4 jit_solution(7571012938556685425)
XLA Ops:
  1.3 6.1 concatenate.7
  8.2 1.6 fusion.28
  9.7 2.9 copy.35
  13.6 4.2 copy.40
  17.8 2.6 subtract_convert_fusion
  20.5 129.2 %shard_map.305 = (f32[4,2,2,2,8,128]{5,4,3,2,1,0:T(8,128)}, bf16[4,2,2,2,32,1024]{5,4,3,2,1,0:T(8,128)(2,1)}, bf16[4,2,2,2,32,1024]{5,4,3,2,1,0:T(8,128)(2,1)}, ...) custom-call(f32[8,128]{1,0:T(8,128)} %pad_convert_fusion.refs_0_, ...), custom_call_target="tpu_custom_call" | custom-call | tf_op jit(solution)/shard_map/pallas_call | solution.py:324
  149.6 0.9 convert.25
  151.0 0.7 reshape.387
  151.8 5.8 add_convert_fusion.3
  157.7 4.1 add_convert_fusion.2
  161.8 4.1 convolution_convert_fusion.7
  165.9 19.7 %fusion.45 = (f32[8,1024]{1,0:T(8,128)S(1)}, f32[8,1024,1024]{1,2,0:T(8,128)}) fusion(f32[1024,1024]{0,1:T(8,128)} %subtract_convert_fusion, f32[8]{0:T(128)S(1)} %multiply_exponential_fusion, bf16[1024,8,128]{0,2,1:T(8,128)(2,1)} %bitcast.92, bf16[1024,8,128]{0,2,1:T(8,128)(2,1)} %bitcast.104, pred[1024,1024]{0,1:T(8,128)(4,1)} %fusion.28), kind=kOutput, calls=%fused_computation.110 | convolution fusion | flops 2189418496 | bytes 43024416 | tf_op jit(solution)/shard_map/qhd,khd->hqk/dot_general | solution.py:555
  185.6 13.2 %fusion = f32[8,1024]{1,0:T(8,128)S(1)} fusion(f32[8,1024,1024]{1,2,0:T(8,128)} %get-tuple-element.89, f32[8,1024]{1,0:T(8,128)S(1)} %get-tuple-element.88), kind=kLoop, calls=%fused_computation.6 | loop fusion | flops 16769024 | bytes 33619968 | tf_op jit(solution)/shard_map/reduce_sum | solution.py:615
  199.4 15.0 %fusion.32 = bf16[8,128,1024]{2,1,0:T(8,128)(2,1)} fusion(bf16[1024,8,128]{0,2,1:T(8,128)(2,1)S(1)} %bitcast.100, f32[8,1024,1024]{1,2,0:T(8,128)} %get-tuple-element.89, f32[8,1024]{1,0:T(8,128)S(1)} %fusion, f32[8,1024]{1,0:T(8,128)S(1)} %get-tuple-element.88), kind=kOutput, calls=%fused_computation.70 | convolution fusion | flops 2173698048 | bytes 37814272 | tf_op jit(solution)/shard_map/hqk,khd->qhd/dot_general | solution.py:618
  214.5 5.0 fusion.46
  220.0 20.2 %multiply_convert_fusion.1 = (bf16[1024,4096]{1,0:T(8,128)(2,1)}, f32[1024,4096]{1,0:T(8,128)}) fusion(f32[4096]{0:T(1024)S(1)} %fusion.33, bf16[1024,4096]{1,0:T(8,128)(2,1)} %bitcast.115, f32[1024,1024]{0,1:T(8,128)S(1)} %get-tuple-element.91, f32[1024]{0:T(1024)S(1)} %reshape.385, f32[1024]{0:T(1024)S(1)} %reshape.384, f32[1024]{0:T(1024)S(1)} %add_rsqrt_fusion, ...), kind=kOutput, calls=%fused_computation.18 | convolution fusion | flops 8620343296 | bytes 37781504 | tf_op jit(solution)/shard_map/dot_general | solution.py:629
  240.2 19.3 %convert_reduce_fusion = (f32[4096]{0:T(1024)}, bf16[1024,4096]{1,0:T(8,128)(2,1)}) fusion(f32[1024,4096]{1,0:T(8,128)} %get-tuple-element.104, f32[4096]{0:T(1024)S(1)} %fusion.33, bf16[4096,1024]{1,0:T(8,128)(2,1)} %bitcast.117, bf16[1024,1024]{1,0:T(8,128)(2,1)S(1)} %copy-done.14), kind=kOutput, calls=%fused_computation.16 | convolution fusion | flops 8644456448 | bytes 35684352 | tf_op jit(solution)/shard_map/td,fd->tf/dot_general | solution.py:698
  259.5 15.0 %add_convert_fusion = bf16[1024,1024]{0,1:T(8,128)(2,1)} fusion(f32[1024,1024]{0,1:T(8,128)S(1)} %get-tuple-element.91, f32[1024]{0:T(1024)S(1)} %copy-done.25, bf16[1024,4096]{1,0:T(8,128)(2,1)} %get-tuple-element.103, bf16[4096,1024]{1,0:T(8,128)(2,1)} %bitcast.118), kind=kOutput, calls=%fused_computation.52 | convolution fusion | flops 8593080320 | bytes 23072768 | tf_op jit(solution)/shard_map/dot_general | solution.py:636
  274.5 15.7 %fusion.47 = (f32[1024]{0:T(1024)}, f32[1024,1024]{1,0:T(8,128)}) fusion(bf16[1024,4096]{1,0:T(8,128)(2,1)} %get-tuple-element.102, bf16[1024,4096]{1,0:T(8,128)(2,1)} %bitcast.116), kind=kOutput, calls=%fused_computation.112 | convolution fusion | flops 8590982144 | bytes 20975616 | tf_op jit(solution)/shard_map/tf,df->td/dot_general | solution.py:706
  290.1 15.0 %convolution_convert_fusion.1 = bf16[4096,1024]{1,0:T(8,128)(2,1)} fusion(bf16[1024,4096]{1,0:T(8,128)(2,1)} %get-tuple-element.103, bf16[1024,1024]{1,0:T(8,128)(2,1)S(1)} %copy-done.14), kind=kOutput, calls=%fused_computation.22 | convolution fusion | flops 8594128896 | bytes 18874368 | tf_op jit(solution)/shard_map/tf,td->fd/dot_general | solution.py:695
  305.2 3.9 copy.51
  309.1 5.3 copy.41
  314.4 5.4 multiply_reduce_fusion.1
  319.9 15.0 %convolution_convert_fusion = bf16[1024,4096]{1,0:T(8,128)(2,1)} fusion(bf16[1024,4096]{1,0:T(8,128)(2,1)} %get-tuple-element.102, f32[1024,1024]{0,1:T(8,128)S(1)} %copy-done.1, f32[1024]{0:T(1024)S(1)} %reshape.385, f32[1024]{0:T(1024)S(1)} %reshape.384, f32[1024]{0:T(1024)S(1)} %add_rsqrt_fusion, f32[1024]{0:T(1024)S(1)} %broadcast_multiply_fusion.4), kind=kOutput, calls=%fused_computation.21 | convolution fusion | flops 8599371776 | bytes 20987904 | tf_op jit(solution)/shard_map/td,tf->df/dot_general | solution.py:703
  334.9 3.0 convert_reduce_fusion.3
  338.0 3.7 convolution_convert_fusion.6
  341.7 3.7 convolution_convert_fusion.2
  345.3 15.7 %convert_reduce_fusion.4 = (f32[8,128]{1,0:T(8,128)S(1)}, bf16[8,128,1024]{2,1,0:T(8,128)(2,1)}) fusion(bf16[1024,8,128]{0,2,1:T(8,128)(2,1)} %bitcast.88, f32[8,1024,1024]{1,2,0:T(8,128)} %get-tuple-element.89, f32[8,1024]{1,0:T(8,128)S(1)} %copy-done.11), kind=kOutput, calls=%fused_computation.46 | convolution fusion | flops 2167405568 | bytes 37785600 | tf_op jit(solution)/shard_map/hqk,qhd->khd/dot_general | solution.py:725
  361.1 5.5 convolution_convert_fusion.3
  366.5 22.2 %multiply_reduce_fusion = (f32[8,1024]{1,0:T(8,128)S(1)}, f32[8,1024,1024]{1,2,0:T(8,128)}) fusion(f32[8,1024,1024]{1,2,0:T(8,128)} %get-tuple-element.89, f32[8,1024]{1,0:T(8,128)S(1)} %copy-done.11, bf16[1024,8,128]{0,2,1:T(8,128)(2,1)S(1)} %bitcast.89, bf16[1024,8,128]{0,2,1:T(8,128)(2,1)S(1)} %bitcast.101), kind=kOutput, calls=%fused_computation.1 | convolution fusion | flops 2172641280 | bytes 71368704 | tf_op jit(solution)/shard_map/qhd,khd->hqk/dot_general | solution.py:724
  388.7 28.3 %multiply_convert_fusion = bf16[8,1024,1024]{1,2,0:T(8,128)(2,1)} fusion(f32[8,1024,1024]{1,2,0:T(8,128)} %get-tuple-element.93, f32[8,1024,1024]{1,2,0:T(8,128)} %get-tuple-element.89, f32[8,1024]{1,0:T(8,128)S(1)} %get-tuple-element.92, f32[8,1024]{1,0:T(8,128)S(1)} %copy-done.11), kind=kLoop, calls=%fused_computation | loop fusion | flops 33554432 | bytes 83951616 | tf_op jit(solution)/shard_map/convert_element_type | solution.py:730
  417.1 13.4 %multiply_convert_fusion.2 = bf16[8,128,1024]{2,1,0:T(8,128)(2,1)} fusion(bf16[1024,8,128]{0,2,1:T(8,128)(2,1)} %bitcast.93, bf16[8,1024,1024]{1,2,0:T(8,128)(2,1)} %multiply_convert_fusion), kind=kOutput, calls=%fused_computation.49 | convolution fusion | flops 2149580800 | bytes 20971520 | tf_op jit(solution)/shard_map/hqk,qhd->khd/dot_general | solution.py:737
  430.5 8.9 %convert_reduce_fusion.5 = (f32[8,128]{1,0:T(8,128)S(1)}, bf16[8,128,1024]{2,1,0:T(8,128)(2,1)S(1)}) fusion(bf16[1024,8,128]{0,2,1:T(8,128)(2,1)} %bitcast.105, bf16[8,1024,1024]{1,2,0:T(8,128)(2,1)} %multiply_convert_fusion), kind=kOutput, calls=%fused_computation.47 | convolution fusion | flops 2151676928 | bytes 20975616 | tf_op jit(solution)/shard_map/hqk,khd->qhd/dot_general | solution.py:733
  439.4 3.8 convolution_convert_fusion.5
  443.2 2.3 fusion.48
  445.6 4.0 convolution_convert_fusion.4
  449.6 2.4 fusion.49
  452.0 3.4 fusion.25
  455.5 2.6 fusion.24
  458.1 4.0 copy.52
  462.8 140.2 %shard_map.306 = (f32[16,1024]{1,0:T(8,128)}, f32[128,1024]{1,0:T(8,128)}, f32[32,4096]{1,0:T(8,128)}, f32[32,1024]{1,0:T(8,128)}, f32[32,1024]{1,0:T(8,128)}, /*index=5*/f32[32,1024]{1,0:T(8,128)}, f32[32,1024]{1,0:T(8,128)}) custom-call(f32[16,1024]{1,0:T(8,128)} %pad.12.refs_0_, bf16[4,2,2,2,128,1024]{5,4,3,2,1,0:T(8,128)(2,1)} %bitcast.90, ...), custom_call_target="tpu_custom_call" | custom-call | tf_op jit(solution)/shard_map/pallas_call | solution.py:373
  603.1 0.9 copy.66
  605.1 1.6 copy.84
  606.7 1.6 copy.85
  608.2 1.6 copy.86
  609.8 1.6 copy.87
  611.4 1.9 copy.88
  613.2 1.9 copy.89
  (105 shorter events, 5.5 us)
Async XLA Ops:
  12.6 201.9 %copy-start.3 = (bf16[1024,1024]{0,1:T(8,128)(2,1)}, bf16[1024,1024]{0,1:T(8,128)(2,1)S(1)}, u32[]{:S(2)}) copy-start(bf16[1024,1024]{0,1:T(8,128)(2,1)S(1)} %copy.35) | copy-start | bytes 6291460
  13.0 148.8 %copy-start.15 = (f32[1024]{0:T(1024)}, f32[1024]{0:T(1024)S(1)}, u32[]{:S(2)}) copy-start(f32[1024]{0:T(1024)S(1)} %broadcast_multiply_fusion.5) | copy-start | bytes 12292
  13.6 148.2 %copy-start.20 = (f32[1024]{0:T(1024)}, f32[1024]{0:T(1024)S(1)}, u32[]{:S(2)}) copy-start(f32[1024]{0:T(1024)S(1)} %add_rsqrt_fusion.1) | copy-start | bytes 12292
  150.8 11.0 %copy-start.18 = (f32[1024]{0:T(1024)}, f32[1024]{0:T(1024)S(1)}, u32[]{:S(2)}) copy-start(f32[1024]{0:T(1024)S(1)} %reshape.379) | copy-start | bytes 12292
  150.9 10.9 %copy-start.23 = (f32[1024]{0:T(1024)}, f32[1024]{0:T(1024)S(1)}, u32[]{:S(2)}) copy-start(f32[1024]{0:T(1024)S(1)} %reshape.380) | copy-start | bytes 12292
  151.8 5.8 copy-start.30
  157.7 4.1 copy-start.28
  185.6 13.8 %copy-start.12 = (bf16[1024,1024]{0,1:T(8,128)(2,1)S(1)}, bf16[1024,1024]{0,1:T(8,128)(2,1)}, u32[]{:S(2)}) copy-start(bf16[1024,1024]{0,1:T(8,128)(2,1)} %add_convert_fusion.3) | copy-start | bytes 6291460
  219.5 40.0 %copy-start = (f32[1024,1024]{0,1:T(8,128)}, f32[1024,1024]{0,1:T(8,128)S(1)}, u32[]{:S(2)}) copy-start(f32[1024,1024]{0,1:T(8,128)S(1)} %get-tuple-element.91) | copy-start | bytes 12582916
  220.0 20.2 %copy-start.14 = (bf16[1024,1024]{1,0:T(8,128)(2,1)S(1)}, bf16[1024,1024]{1,0:T(8,128)(2,1)}, u32[]{:S(2)}) copy-start(bf16[1024,1024]{1,0:T(8,128)(2,1)} %param.19) | copy-start | bytes 6291460
  240.2 19.3 %copy-start.25 = (f32[1024]{0:T(1024)S(1)}, f32[1024]{0:T(1024)}, u32[]{:S(2)}) copy-start(f32[1024]{0:T(1024)} %reshape.387) | copy-start | bytes 12292
  314.4 5.4 copy-start.1
  319.9 15.0 %copy-start.2 = (f32[1024,1024]{0,1:T(8,128)S(1)}, f32[1024,1024]{0,1:T(8,128)}, u32[]{:S(2)}) copy-start(f32[1024,1024]{0,1:T(8,128)} %copy.41) | copy-start | bytes 12582916
  319.9 15.0 %copy-start.8 = (bf16[1024,1024]{0,1:T(8,128)(2,1)S(1)}, bf16[1024,1024]{0,1:T(8,128)(2,1)}, u32[]{:S(2)}) copy-start(bf16[1024,1024]{0,1:T(8,128)(2,1)} %copy.40) | copy-start | bytes 6291460
  334.9 3.0 copy-start.33
  337.9 3.7 copy-start.5
  338.0 3.7 copy-start.32
  341.7 3.7 copy-start.11
  345.3 15.7 %copy-start.4 = (bf16[1024,1024]{0,1:T(8,128)(2,1)S(1)}, bf16[1024,1024]{0,1:T(8,128)(2,1)}, u32[]{:S(2)}) copy-start(bf16[1024,1024]{0,1:T(8,128)(2,1)} %copy-done.3) | copy-start | bytes 6291460
  345.3 15.7 %copy-start.16 = (f32[1024]{0:T(1024)S(1)}, f32[1024]{0:T(1024)}, u32[]{:S(2)}) copy-start(f32[1024]{0:T(1024)} %copy-done.15) | copy-start | bytes 12292
  345.3 15.7 %copy-start.19 = (f32[1024]{0:T(1024)S(1)}, f32[1024]{0:T(1024)}, u32[]{:S(2)}) copy-start(f32[1024]{0:T(1024)} %copy-done.18) | copy-start | bytes 12292
  345.3 15.7 %copy-start.21 = (f32[1024]{0:T(1024)S(1)}, f32[1024]{0:T(1024)}, u32[]{:S(2)}) copy-start(f32[1024]{0:T(1024)} %copy-done.20) | copy-start | bytes 12292
  345.3 15.7 %copy-start.24 = (f32[1024]{0:T(1024)S(1)}, f32[1024]{0:T(1024)}, u32[]{:S(2)}) copy-start(f32[1024]{0:T(1024)} %copy-done.23) | copy-start | bytes 12292
  361.1 5.5 copy-start.7
  361.1 5.5 copy-start.13
  439.4 3.8 copy-start.31
  443.2 2.4 copy-start.9
  445.6 4.0 copy-start.29
  449.6 2.4 copy-start.10
  449.6 2.4 copy-start.27
  452.0 3.5 copy-start.6
  458.1 4.0 copy-start.17
  458.1 4.0 copy-start.26
  458.1 4.1 copy-start.22

commit v2 on v1

--- a/solution.py
+++ b/solution.py
@@ -513,6 +513,319 @@
         lax.psum_scatter(down_weight, ("wide", "narrow"), scatter_dimension=0, tiled=True),
         lax.psum_scatter(down_bias, ("wide", "narrow"), scatter_dimension=0, tiled=True),
     )
+
+
+LOG2E = 1.4426950408889634
+WEIGHTS = ("query", "key", "value", "out", "up", "down")
+
+
+def dot(left, right, form):
+    dims = (((0,) if form[0] == "T" else (1,), (1,) if form[1] == "T" else (0,)), ((), ()))
+    return lax.dot_general(left, right, dims, preferred_element_type=F32)
+
+
+def at(index, size):
+    return pl.ds(pl.multiple_of(index * size, size), size)
+
+
+def loop(count, body):
+    def step(i, carry):
+        body(i)
+        return carry
+
+    lax.fori_loop(0, count, step, 0)
+
+
+def normed_rows(value):
+    center = value - jnp.mean(value, -1, keepdims=True)
+    inverse = lax.rsqrt(jnp.mean(center * center, -1, keepdims=True) + EPSILON)
+    return center * inverse, inverse
+
+
+def gelu_pair(hidden):
+    cdf = 0.5 * (1.0 + lax.erf(hidden * 0.7071067811865476))
+    density = jnp.exp2(hidden * hidden * (-0.5 * LOG2E)) * 0.3989422804014327
+    return hidden * cdf, cdf + hidden * density
+
+
+def unpack_small(small, vec):
+    table = small.reshape(256, 128)
+    values = table[...].astype(BF)
+    lane = lax.broadcasted_iota(jnp.int32, (128, 1024), 0)
+    column = lax.broadcasted_iota(jnp.int32, (128, 1024), 1)
+    row = lax.broadcasted_iota(jnp.int32, (256, 1024), 0)
+    owner = lax.div(lax.broadcasted_iota(jnp.int32, (256, 1024), 1), 32) * 8
+    for part in range(4):
+        pick = jnp.where(lane == part * 32 + lax.rem(column, 32), 1.0, 0.0).astype(BF)
+        spread_out = dot(values, pick, "NN")
+        for line in range(2):
+            chosen = jnp.where(row == owner + line, spread_out, 0.0)
+            index = line * 4 + part
+            vec[index : index + 1, :] = jnp.sum(chosen, 0, keepdims=True)
+    for part in range(4):
+        for block in range(8):
+            source = (part * 8 + block) * 8 + 2
+            vec[8 + part : 9 + part, block * 128 : block * 128 + 128] = table[source : source + 1, :]
+
+
+def prepare_bias(length, mask, ramp):
+    key = lax.broadcasted_iota(jnp.int32, (256, 256), 0)
+    query = lax.broadcasted_iota(jnp.int32, (256, 256), 1)
+    long = length == 1024
+    same = (lax.div(key, 128) == lax.div(query, 128)) | long
+    mask[...] = jnp.where((key <= query) & same, 0.0, -1e30)
+    ramp[...] = lax.broadcasted_iota(jnp.int32, (1024, 128), 0).astype(F32)
+    return jnp.where(long, 0.0, -1e30)
+
+
+def wide(value):
+    return jnp.concatenate([value, value], axis=1)
+
+
+def attention_head(head, slope, off, queries, keys, values, mixed, lse, mask, ramp, tilt):
+    cols = at(head, 128)
+    factor = HD**-0.5 * LOG2E
+    tilt[...] = ramp[...] * slope
+    for i in range(4):
+        rows, before = slice(i * 256, i * 256 + 256), slice(0, i * 256)
+        query = queries[rows, cols]
+        near = dot(keys[rows, cols], query, "NT") * factor + wide(tilt[rows, :]) + mask[...]
+        top = jnp.max(near, 0, keepdims=True)
+        if i:
+            past = dot(keys[before, cols], query, "NT") * factor + wide(tilt[before, :])
+            top = jnp.maximum(top, jnp.max(past, 0, keepdims=True) + off)
+        near = jnp.exp2(near - top)
+        total = jnp.sum(near, 0, keepdims=True)
+        out = dot(values[rows, cols], near.astype(BF), "TN")
+        if i:
+            past = jnp.exp2(past + (off - top))
+            total = total + jnp.sum(past, 0, keepdims=True)
+            out = out + dot(values[before, cols], past.astype(BF), "TN")
+        mixed[rows, cols] = (out * (1.0 / total)).T.astype(BF)
+        lse[pl.ds(head, 1), rows] = top + jnp.log2(total)
+
+
+def forward_kernel(length_ref, tokens, *refs):
+    refs = list(refs)
+
+    def take(count):
+        taken, refs[:count] = refs[:count], []
+        return taken
+
+    local = take(7)
+    result_out, resid_out, lse_out, small_out = take(4)
+    attn_out, query_out, key_out, value_out, mixed_out, ffn_out, active_out, slope_out = take(8)
+    weight_out = take(6)
+    full = take(7)
+    act, slope, mixed, ffn_in = take(4)
+    resid, vec, lse, mask, ramp, tilt = take(6)
+    send, recv, keep, store, dump = take(5)
+
+    place = Place()
+    place.greet()
+    tasks, dumps = [], []
+    for i, cut in enumerate((1, 1, 1, 1, 1, 4, 4)):
+        width = local[i].shape[-1] // cut
+        for j in range(cut):
+            g = len(tasks)
+            views = [halves(ref, cut, width)[j] for ref in (local[i], full[i])]
+            tasks.append(Gathering(place, *views, send.at[g], recv.at[g], keep.at[g]))
+            if i:
+                target = halves(weight_out[i - 1], cut, width)[j]
+                dumps.append(pltpu.make_async_copy(views[1], target, dump.at[g - 1]))
+
+    def tick(number):
+        for stage in reversed(range(Gathering.STAGES)):
+            g = number - stage
+            if 0 <= g < len(tasks):
+                tasks[g].stage(stage)
+                if stage == Gathering.STAGES - 1 and g:
+                    dumps[g - 1].start()
+
+    saves = []
+
+    def save(source, target):
+        copy = pltpu.make_async_copy(source, target, store.at[len(saves)])
+        copy.start()
+        saves.append(copy)
+
+    query_w, key_w, value_w, out_w = (ref.reshape(1024, 1024) for ref in full[1:5])
+    up_w, down_w = full[5].reshape(1024, 4096), full[6].reshape(4096, 1024)
+    attn_in, queries, keys, values = (act.at[i] for i in range(4))
+    length = length_ref[0]
+    off = prepare_bias(length, mask, ramp)
+
+    for number in range(5):
+        tick(number)
+    unpack_small(full[0], vec)
+
+    def first_norm(i):
+        rows = at(i, 128)
+        normed, _ = normed_rows(tokens[rows, :].astype(F32))
+        attn_in[rows, :] = (normed * vec[0:1, :] + vec[1:2, :]).astype(BF)
+
+    loop(8, first_norm)
+    save(attn_in, attn_out)
+
+    def project(weight, target, bias):
+        def body(i):
+            cols = at(i, 512)
+            value = dot(attn_in[...], weight[:, cols], "NN")
+            if bias is not None:
+                value = value + vec[bias : bias + 1, cols]
+            target[:, cols] = value.astype(BF)
+
+        loop(2, body)
+
+    tick(5)
+    project(query_w, queries, 2)
+    save(queries, query_out)
+    tick(6)
+    project(key_w, keys, None)
+    save(keys, key_out)
+    tick(7)
+    project(value_w, values, 3)
+    save(values, value_out)
+
+    def heads(first):
+        def body(i, slope_now):
+            attention_head(
+                first + i, slope_now, off, queries, keys, values, mixed, lse, mask, ramp, tilt
+            )
+            return slope_now * 0.5
+
+        lax.fori_loop(0, 2, body, jnp.float32(LOG2E * 0.5 ** (first + 1)))
+
+    for pair in range(4):
+        heads(2 * pair)
+        if pair < 3:
+            tick(8 + pair)
+    save(mixed, mixed_out)
+    save(lse, lse_out)
+
+    def close_attention(i):
+        rows = at(i, 256)
+        value = dot(mixed[rows, :], out_w[...], "NN") + tokens[rows, :].astype(F32) + vec[4:5, :]
+        resid[rows, :] = value
+        normed, _ = normed_rows(value)
+        ffn_in[rows, :] = (normed * vec[5:6, :] + vec[6:7, :]).astype(BF)
+
+    loop(4, close_attention)
+    save(resid, resid_out)
+    save(ffn_in, ffn_out)
+    for copy in saves[:5]:
+        copy.wait()
+
+    def widen(chunk):
+        def body(i):
+            rows, cols = at(lax.div(i, 2), 512), at(lax.rem(i, 2), 512)
+            weight = up_w[:, at(chunk * 2 + lax.rem(i, 2), 512)]
+            hidden = dot(ffn_in[rows, :], weight, "NN") + vec[8 + chunk : 9 + chunk, cols]
+            active, steep = gelu_pair(hidden)
+            act[chunk, rows, cols] = active.astype(BF)
+            slope[chunk, rows, cols] = steep.astype(BF)
+
+        loop(4, body)
+        save(act.at[chunk], active_out.at[chunk])
+        save(slope.at[chunk], slope_out.at[chunk])
+
+    widen(0)
+    widen(1)
+    tick(11)
+    widen(2)
+    tick(12)
+    widen(3)
+
+    def narrow(chunk):
+        cols = slice(chunk * 256, chunk * 256 + 256)
+
+        def body(i):
+            rows = at(i, 512)
+            value = resid[rows, cols] + vec[7:8, cols]
+            active = jnp.concatenate([act[j, rows, :] for j in range(4)], axis=1)
+            value = value + dot(active, down_w[:, cols], "NN")
+            mixed[rows, cols] = value.astype(BF)
+
+        loop(2, body)
+
+    for chunk in range(4):
+        tick(13 + chunk)
+        narrow(chunk)
+    save(mixed, result_out)
+    small_out[...] = vec[...]
+    for task in tasks:
+        task.finish()
+    for copy in saves[5:]:
+        copy.wait()
+    for copy in dumps:
+        copy.wait()
+
+
+def forward_all(length, tokens, flat, weights):
+    square = jax.ShapeDtypeStruct((1024, 1024), BF)
+    tall = jax.ShapeDtypeStruct((4, 1024, 1024), BF)
+    f32 = functools.partial(jax.ShapeDtypeStruct, dtype=F32)
+    grid6 = [(4, 2, 2, 2) + w.shape for w in weights]
+    hbm, vmem = pl.BlockSpec(memory_space=pltpu.HBM), pl.BlockSpec(memory_space=pltpu.VMEM)
+    return pl.pallas_call(
+        forward_kernel,
+        out_shape=[square, f32((1024, 1024)), f32((8, 1024)), f32((16, 1024))]
+        + [square] * 6
+        + [tall] * 2
+        + [jax.ShapeDtypeStruct(s, BF) for s in grid6],
+        in_specs=[pl.BlockSpec(memory_space=pltpu.SMEM)] + [vmem] * 8,
+        out_specs=[hbm, hbm, hbm, vmem] + [hbm] * 14,
+        scratch_shapes=[pltpu.VMEM((4, 2, 2, 2) + flat.shape, F32)]
+        + [pltpu.VMEM(s, BF) for s in grid6]
+        + [pltpu.VMEM((4, 1024, 1024), BF)] * 2
+        + [pltpu.VMEM((1024, 1024), BF)] * 2
+        + [
+            pltpu.VMEM((1024, 1024), F32),
+            pltpu.VMEM((16, 1024), F32),
+            pltpu.VMEM((8, 1024), F32),
+            pltpu.VMEM((256, 256), F32),
+            pltpu.VMEM((1024, 128), F32),
+            pltpu.VMEM((1024, 128), F32),
+            pltpu.SemaphoreType.DMA((13, Gathering.SEMS)),
+            pltpu.SemaphoreType.DMA((13, Gathering.SEMS)),
+            pltpu.SemaphoreType.DMA((13,)),
+            pltpu.SemaphoreType.DMA((17,)),
+            pltpu.SemaphoreType.DMA((12,)),
+        ],
+        compiler_params=pltpu.CompilerParams(
+            collective_id=2, has_side_effects=True, vmem_limit_bytes=60 << 20
+        ),
+    )(length, tokens, flat, *weights)
+
+
+def pack_small(parts):
+    flat = jnp.concatenate([parts[i].astype(F32) for i in SMALL]).reshape(-1, 128)
+    return jnp.pad(flat, ((0, 8 - flat.shape[0]), (0, 0)))
+
+
+def forward_fast(tokens, seq_length, parts):
+    out = forward_all(seq_length, tokens, pack_small(parts), [parts[i] for i in LARGE])
+    result, resid, lse, vec, attn_in, queries, keys, values, mixed, ffn_in, active, slope = out[:12]
+    large = out[12:]
+    whole = [None] * 15
+    for row, i in enumerate((0, 1, 3, 6, 8, 9, 10, 14)):
+        whole[i] = vec[row].astype(BF)
+    whole[12] = vec[8:12].reshape(-1).astype(BF)
+    for i, array in zip(LARGE, large):
+        whole[i] = array.reshape(-1, array.shape[-1])
+    count = tokens.shape[0]
+    center = tokens.astype(F32)
+    center = center - jnp.mean(center, -1, keepdims=True)
+    inv1 = lax.rsqrt(jnp.mean(center * center, -1, keepdims=True) + EPSILON)
+    c2 = resid - jnp.mean(resid, -1, keepdims=True)
+    inv2 = lax.rsqrt(jnp.mean(c2 * c2, -1, keepdims=True) + EPSILON)
+    slopes = jnp.exp2(-8.0 * jnp.arange(1, H + 1, dtype=F32) / H)
+    natural = lse / LOG2E - slopes[:, None] * jnp.arange(count, dtype=F32)[None]
+    flat4 = lambda a: a.transpose(1, 0, 2).reshape(count, -1)
+    kept = (result, attn_in, center * inv1, inv1) + tuple(
+        a.reshape(count, H, HD) for a in (queries, keys, values)
+    ) + (natural[:, :, None], mixed, c2 * inv2, inv2, ffn_in, flat4(slope).astype(F32), flat4(active))
+    return tuple(whole), kept
 
 
 def is_fast():
@@ -822,8 +1135,11 @@
         down_bias,
     )
     length = seq_length[0]
-    weights = collect(shards)
-    kept = forward(tokens, length, weights)
+    if is_fast():
+        weights, kept = forward_fast(tokens, seq_length, shards)
+    else:
+        weights = collect(shards)
+        kept = forward(tokens, length, weights)
     grad_tokens, sums = backward(cotangent, length, weights, kept)
     (
         g_first_gain,

time: 622 us -> 610 us (0.981)
  matrix products: 243 us -> 176 us
  local copies, waits for them, and re-layouts: 40.5 us -> 69.5 us
  Pallas kernels: 269 us -> 294 us
    dot_general x7 -> x0, matrix products: 69.2 us -> none  [the longest x1 20.2 us: forward(): jnp.dot(ffn_in, up_weight, preferred_element_type=jnp.float32)]
    convert_element_type x8 -> x2, local copies, waits for them, and re-layouts: 1.17 us -> 34 us  [forward_fast(): flat4(slope).astype(F32)]
    pallas_call x1, Pallas kernels: 129 us -> 148 us  [forward_all(): pl.pallas_call(forward_kernel, out_shape=[square, f32((1024, 1024)), f32(...]
    unnamed x88 -> x76, local copies, waits for them, and re-layouts: 26 us -> 7.68 us
    reduce_sum x5 -> x4, other arithmetic: 20.1 us -> 6.22 us  [the longest x1 2.74 us: forward_fast(): inv2 = lax.rsqrt(jnp.mean(c2 * c2, -1, keepdims=True) + EPSILON)]
    transpose x0 -> x1, local copies, waits for them, and re-layouts: none -> 11.4 us  [forward_fast(): flat4 = lambda a: a.transpose(1, 0, 2).reshape(count, -1)]
    convert_element_type x2 -> x1, other arithmetic: 0.09 us -> 11.3 us  [forward_fast(): flat4(slope).astype(F32)]
    reshape x0 -> x2, local copies, waits for them, and re-layouts: none -> 8.54 us  [forward_fast(): a.reshape(count, H, HD)]
where the time goes in v2:
time: 610 us; the launch traced here: 600 us
  Pallas kernels  294 us (48%)
  matrix products  176 us (29%)
  local copies, waits for them, and re-layouts  69.5 us (11%)
  other arithmetic  58.1 us (10%)
    pallas_call x1, Pallas kernels, forward_all(): pl.pallas_call(forward_kernel, out_shape=[square, f32((1024, 1024)), f32(...  148 us
    pallas_call x1, Pallas kernels, scatter_all(): pl.pallas_call(functools.partial(scatter_kernel, cuts), out_shape=[jax.Sh...  146 us
    convert_element_type x2, local copies, waits for them, and re-layouts, forward_fast(): flat4(slope).astype(F32)  34 us
    convert_element_type x1, other arithmetic, backward(): grad_scores = (probs * (grad_probs - row_total)).astype(jnp.bfloat16)  28.4 us
    dot_general x1, matrix products, backward(): jnp.einsum('qhd,khd->hqk', grad_mixed, values, preferred_element_type=jnp...  22 us
    dot_general x1, matrix products, masked_scores(): jnp.einsum('qhd,khd->hqk', queries, keys, preferred_element_type=jnp.floa...  19.8 us
    dot_general x1, matrix products, backward(): jnp.einsum('td,fd->tf', cotangent, down_weight, preferred_element_type=jn...  17.3 us
    dot_general x1, matrix products, backward(): jnp.einsum('hqk,qhd->khd', probs.astype(jnp.bfloat16), grad_mixed, prefer...  15.6 us

profile of v2, /device:TPU:2, one launch (start us, length us, event | category | flops | bytes accessed | tf_op | source)
XLA Modules:
  0.0 600.4 jit_solution(3482466089891118145)
XLA Ops:
  1.3 6.1 %concatenate.7 = bf16[384]{0:T(512)(128)(2,1)S(1)} concatenate(bf16[32]{0:T(256)(128)(2,1)} %param.21, bf16[32]{0:T(256)(128)(2,1)} %param.22, bf16[32]{0:T(256)(128)(2,1)} %param.24, bf16[32]{0:T(256)(128)(2,1)} %param.27, bf16[32]{0:T(256)(128)(2,1)} %param.29, bf16[32]{0:T(256)(128)(2,1)} %param.30, bf16[32]{0:T(256)(128)(2,1)} %param.31, bf16[32]{0:T(256)(128)(2,1)} %param.35, ...), dimensions={0} | concatenate | bytes 1536 | tf_op jit(solution)/shard_map/concatenate | solution.py:802
  7.4 0.6 pad_convert_fusion.refs_0_
  8.0 147.9 %shard_map.305 = (bf16[1024,1024]{1,0:T(8,128)(2,1)}, f32[1024,1024]{1,0:T(8,128)}, f32[8,1024]{1,0:T(8,128)}, f32[16,1024]{1,0:T(8,128)}, bf16[1024,1024]{1,0:T...) custom-call(s32[1]{0:T(128)} %copy.85.length_ref, ...), custom_call_target="tpu_custom_call" | custom-call | tf_op jit(solution)/shard_map/pallas_call | solution.py:770
  155.9 2.5 reduce_sum.166
  158.4 2.7 multiply_reduce_fusion.3
  161.2 11.3 %convert_bitcast_fusion = f32[1024,4,1024]{2,0,1:T(8,128)} fusion(bf16[4,1024,1024]{2,1,0:T(8,128)(2,1)} %get-tuple-element.45), kind=kLoop, calls=%fused_computation.5 | loop fusion | flops 4194304 | bytes 25165824 | tf_op jit(solution)/shard_map/convert_element_type | solution.py:827
  172.4 16.4 %copy.44 = f32[1024,4,1024]{0,2,1:T(8,128)} copy(f32[1024,4,1024]{2,0,1:T(8,128)} %convert_bitcast_fusion) | data formatting | bytes 33554432 | tf_op jit(solution)/shard_map/convert_element_type | solution.py:827
  188.8 17.6 %copy.45 = f32[1024,4096]{1,0:T(8,128)} copy(f32[1024,4096]{0,1:T(8,128)} %bitcast.86) | data formatting | bytes 33554432 | tf_op jit(solution)/shard_map/convert_element_type | solution.py:827
  206.4 17.3 %convert_reduce_fusion = (f32[4096]{0:T(1024)}, bf16[1024,4096]{1,0:T(8,128)(2,1)}) fusion(f32[1024,4096]{1,0:T(8,128)} %copy.45, bf16[4096,1024]{1,0:T(8,128)(2,1)} %bitcast.116, bf16[1024,1024]{1,0:T(8,128)(2,1)S(1)} %copy-done.10), kind=kOutput, calls=%fused_computation.6 | convolution fusion | flops 8606707712 | bytes 35667968 | tf_op jit(solution)/shard_map/td,fd->tf/dot_general | solution.py:1011
  223.8 0.6 slice_convert_fusion
  224.4 14.9 %multiply_reduce_fusion.1 = (f32[1024]{0:T(1024)S(1)}, f32[1024]{0:T(1024)S(1)}, f32[1024]{0:T(1024)S(1)}, f32[1024]{0:T(1024)S(1)}, f32[1024,1024]{1,0:T(8,128)S(1)}) fusion(f32[1024,1024]{1,0:T(8,128)S(1)} %copy-done, f32[1024]{0:T(1024)S(1)} %add_rsqrt_fusion.1, f32[1024]{0:T(1024)S(1)} %broadcast_multiply_fusion.5, f32[1024]{0:T(1024)S(1)} %bitcast.112, ...), kind=kOutput, calls=%fused_computation.27 | convolution fusion | flops 8599367680 | bytes 25194496 | tf_op jit(solution)/shard_map/tf,df->td/dot_general | solution.py:1019
  239.4 2.2 convert_reduce_fusion.3
  241.6 2.4 convolution_convert_fusion.6
  244.1 4.6 copy.60
  248.7 3.9 copy.61
  252.8 0.6 fusion.15
  253.4 2.6 subtract_convert_fusion
  256.1 19.8 %subtract_exponential_fusion = f32[8,1024,1024]{1,2,0:T(8,128)} fusion(f32[8,1024]{1,0:T(8,128)S(1)} %multiply_subtract_fusion, f32[1024,1024]{0,1:T(8,128)} %subtract_convert_fusion, f32[8]{0:T(128)S(1)} %multiply_exponential_fusion, pred[1024,1024]{0,1:T(8,128)(4,1)S(1)} %fusion.15, bf16[1024,8,128]{0,2,1:T(8,128)(2,1)} %bitcast.89, ...), kind=kOutput, calls=%fused_computation.2 | convolution fusion | flops 2189426688 | bytes 43024416 | tf_op jit(solution)/shard_map/qhd,khd->hqk/dot_general | solution.py:868
  275.9 22.0 %multiply_reduce_fusion = (f32[8,1024]{1,0:T(8,128)S(1)}, f32[8,1024,1024]{1,2,0:T(8,128)}) fusion(f32[8,1024,1024]{1,2,0:T(8,128)} %subtract_exponential_fusion, bf16[1024,8,128]{0,2,1:T(8,128)(2,1)S(1)} %bitcast.87, bf16[1024,1024]{1,0:T(8,128)(2,1)} %get-tuple-element.52), kind=kOutput, calls=%fused_computation.1 | convolution fusion | flops 2164252672 | bytes 71335936 | tf_op jit(solution)/shard_map/qhd,khd->hqk/dot_general | solution.py:1037
  297.9 28.4 %multiply_convert_fusion = bf16[8,1024,1024]{1,2,0:T(8,128)(2,1)} fusion(f32[8,1024,1024]{1,2,0:T(8,128)} %subtract_exponential_fusion, f32[8,1024,1024]{1,2,0:T(8,128)} %get-tuple-element.90, f32[8,1024]{1,0:T(8,128)S(1)} %get-tuple-element.89), kind=kLoop, calls=%fused_computation | loop fusion | flops 25165824 | bytes 83918848 | tf_op jit(solution)/shard_map/convert_element_type | solution.py:1043
  326.3 12.8 %multiply_convert_fusion.1 = bf16[8,128,1024]{2,1,0:T(8,128)(2,1)} fusion(bf16[1024,8,128]{0,2,1:T(8,128)(2,1)S(1)} %bitcast.90, bf16[8,1024,1024]{1,2,0:T(8,128)(2,1)} %multiply_convert_fusion), kind=kOutput, calls=%fused_computation.32 | convolution fusion | flops 2149580800 | bytes 20971520 | tf_op jit(solution)/shard_map/hqk,qhd->khd/dot_general | solution.py:1050
  339.0 6.1 %convolution_convert_fusion.3 = bf16[1024,1024]{1,0:T(8,128)(2,1)} fusion(bf16[1024,1024]{1,0:T(8,128)(2,1)} %get-tuple-element.59, bf16[1024,1024]{0,1:T(8,128)(2,1)} %bitcast.97), kind=kOutput, calls=%fused_computation.46 | convolution fusion | flops 2148532224 | bytes 6291456 | tf_op jit(solution)/shard_map/tc,td->cd/dot_general | solution.py:1059
  345.1 8.6 %convert_reduce_fusion.5 = (f32[8,128]{1,0:T(8,128)S(1)}, bf16[8,128,1024]{2,1,0:T(8,128)(2,1)S(1)}) fusion(bf16[1024,8,128]{0,2,1:T(8,128)(2,1)S(1)} %bitcast.96, bf16[8,1024,1024]{1,2,0:T(8,128)(2,1)} %multiply_convert_fusion), kind=kOutput, calls=%fused_computation.30 | convolution fusion | flops 2151676928 | bytes 20975616 | tf_op jit(solution)/shard_map/hqk,khd->qhd/dot_general | solution.py:1046
  353.7 3.7 convolution_convert_fusion.4
  357.4 4.6 fusion.27
  362.1 4.4 fusion.26
  366.4 15.6 %convert_reduce_fusion.4 = (f32[8,128]{1,0:T(8,128)S(1)}, bf16[8,128,1024]{2,1,0:T(8,128)(2,1)}) fusion(bf16[1024,8,128]{0,2,1:T(8,128)(2,1)} %bitcast.88, f32[8,1024,1024]{1,2,0:T(8,128)} %subtract_exponential_fusion), kind=kOutput, calls=%fused_computation.29 | convolution fusion | flops 2159016960 | bytes 37752832 | tf_op jit(solution)/shard_map/hqk,qhd->khd/dot_general | solution.py:1038
  382.4 0.7 fusion.14
  383.6 0.6 copy-done.24
  384.3 7.9 %fusion.13 = (f32[1024]{0:T(1024)S(1)}, f32[1024]{0:T(1024)S(1)}, f32[1024]{0:T(1024)S(1)}, f32[1024]{0:T(1024)S(1)}, f32[1024,1024]{1,0:T(8,128)}) fusion(bf16[1024,1024]{1,0:T(8,128)(2,1)S(1)} %copy-done.1, f32[1024]{0:T(1024)S(1)} %add_rsqrt_fusion, f32[1024]{0:T(1024)S(1)} %broadcast_multiply_fusion.2, f32[1024]{0:T(1024)S(1)} %bitcast.110, ...), kind=kOutput, calls=%fused_computation.25 | convolution fusion | flops 2160062464 | bytes 18903040 | tf_op jit(solution)/shard_map/td,cd->tc/dot_general | solution.py:1071
  392.3 0.6 pad.12.refs_0_
  392.9 6.1 %convolution_convert_fusion.2 = bf16[1024,1024]{1,0:T(8,128)(2,1)} fusion(bf16[1024,1024]{1,0:T(8,128)(2,1)} %get-tuple-element.59, bf16[1024,1024]{0,1:T(8,128)(2,1)} %bitcast.99), kind=kOutput, calls=%fused_computation.45 | convolution fusion | flops 2148532224 | bytes 6291456 | tf_op jit(solution)/shard_map/tc,td->cd/dot_general | solution.py:1062
  399.1 3.8 convolution_convert_fusion.5
  402.9 11.1 %convolution_convert_fusion = bf16[1024,4096]{1,0:T(8,128)(2,1)} fusion(bf16[1024,1024]{1,0:T(8,128)(2,1)S(1)} %copy-done.21, bf16[1024,4096]{1,0:T(8,128)(2,1)S(1)} %bitcast.122), kind=kOutput, calls=%fused_computation.9 | convolution fusion | flops 8594128896 | bytes 18874368 | tf_op jit(solution)/shard_map/td,tf->df/dot_general | solution.py:1016
  414.0 11.4 %copy.55 = bf16[1024,4,1024]{0,2,1:T(8,128)(2,1)} copy(bf16[1024,4,1024]{2,0,1:T(8,128)(2,1)} %bitcast.93) | data formatting | bytes 16777216 | tf_op jit(solution)/shard_map/transpose | solution.py:824
  425.4 15.1 %convolution_convert_fusion.1 = bf16[4096,1024]{1,0:T(8,128)(2,1)} fusion(bf16[1024,4096]{0,1:T(8,128)(2,1)} %bitcast.94, bf16[1024,1024]{1,0:T(8,128)(2,1)} %param.19), kind=kOutput, calls=%fused_computation.10 | convolution fusion | flops 8594128896 | bytes 18874368 | tf_op jit(solution)/shard_map/tf,td->fd/dot_general | solution.py:1008
  440.4 146.5 %shard_map.306 = (f32[16,1024]{1,0:T(8,128)}, f32[128,1024]{1,0:T(8,128)}, f32[32,4096]{1,0:T(8,128)}, f32[32,1024]{1,0:T(8,128)}, f32[32,1024]{1,0:T(8,128)}, /*index=5*/f32[32,1024]{1,0:T(8,128)}, f32[32,1024]{1,0:T(8,128)}) custom-call(f32[16,1024]{1,0:T(8,128)} %pad.12.refs_0_, bf16[4,2,2,2,128,1024]{5,4,3,2,1,0:T(8,128)(2,1)} %bitcast.92, ...), custom_call_target="tpu_custom_call" | custom-call | tf_op jit(solution)/shard_map/pallas_call | solution.py:373
  586.9 0.9 copy.63
  587.8 0.6 fusion.25
  588.4 0.6 dynamic_slice.34
  589.0 5.3 fusion.12
  594.4 1.3 copy.86
  595.7 0.7 copy.87
  596.3 0.7 copy.88
  597.0 0.7 copy.89
  597.7 0.7 copy.90
  598.3 0.8 copy.91
  599.1 0.8 copy.92
  (82 shorter events, 1.3 us)
Async XLA Ops:
  188.8 17.6 %copy-start.10 = (bf16[1024,1024]{1,0:T(8,128)(2,1)S(1)}, bf16[1024,1024]{1,0:T(8,128)(2,1)}, u32[]{:S(2)}) copy-start(bf16[1024,1024]{1,0:T(8,128)(2,1)} %param.19) | copy-start | bytes 6291460
  206.4 17.3 %copy-start.17 = (f32[16,1024]{1,0:T(8,128)S(1)}, f32[16,1024]{1,0:T(8,128)}, u32[]{:S(2)}) copy-start(f32[16,1024]{1,0:T(8,128)} %get-tuple-element.47) | copy-start | bytes 196612
  206.4 18.0 %copy-start = (f32[1024,1024]{1,0:T(8,128)S(1)}, f32[1024,1024]{1,0:T(8,128)}, u32[]{:S(2)}) copy-start(f32[1024,1024]{1,0:T(8,128)} %get-tuple-element.43) | copy-start | bytes 12582916
  239.4 2.3 copy-start.27
  241.6 2.4 copy-start.3
  244.0 31.9 %copy-start.2 = (bf16[1024,1024]{0,1:T(8,128)(2,1)}, bf16[1024,1024]{0,1:T(8,128)(2,1)S(1)}, u32[]{:S(2)}) copy-start(bf16[1024,1024]{0,1:T(8,128)(2,1)S(1)} %convolution_convert_fusion.6) | copy-start | bytes 6291460
  244.0 8.6 %copy-start.18 = (f32[8,1024]{1,0:T(8,128)S(1)}, f32[8,1024]{1,0:T(8,128)}, u32[]{:S(2)}) copy-start(f32[8,1024]{1,0:T(8,128)} %get-tuple-element.50) | copy-start | bytes 98308
  297.9 28.4 %copy-start.5 = (bf16[1024,1024]{0,1:T(8,128)(2,1)S(1)}, bf16[1024,1024]{0,1:T(8,128)(2,1)}, u32[]{:S(2)}) copy-start(bf16[1024,1024]{0,1:T(8,128)(2,1)} %copy.61) | copy-start | bytes 6291460
  339.0 6.1 %copy-start.6 = (bf16[1024,1024]{0,1:T(8,128)(2,1)S(1)}, bf16[1024,1024]{0,1:T(8,128)(2,1)}, u32[]{:S(2)}) copy-start(bf16[1024,1024]{0,1:T(8,128)(2,1)} %copy.60) | copy-start | bytes 6291460
  345.1 8.6 %copy-start.23 = (bf16[1024,1024]{1,0:T(8,128)(2,1)S(1)}, bf16[1024,1024]{1,0:T(8,128)(2,1)}, u32[]{:S(2)}) copy-start(bf16[1024,1024]{1,0:T(8,128)(2,1)} %get-tuple-element.59) | copy-start | bytes 6291460
  353.7 3.7 copy-start.7
  353.7 3.7 copy-start.26
  357.4 4.6 copy-start.25
  366.4 15.6 %copy-start.1 = (bf16[1024,1024]{1,0:T(8,128)(2,1)S(1)}, bf16[1024,1024]{1,0:T(8,128)(2,1)}, u32[]{:S(2)}) copy-start(bf16[1024,1024]{1,0:T(8,128)(2,1)} %tokens.1) | copy-start | bytes 6291460
  382.0 1.6 copy-start.8
  382.0 1.6 copy-start.19
  382.0 2.2 copy-start.24
  384.3 8.0 %copy-start.20 = (f32[4096]{0:T(1024)S(1)}, f32[4096]{0:T(1024)}, u32[]{:S(2)}) copy-start(f32[4096]{0:T(1024)} %get-tuple-element.96) | copy-start | bytes 49156
  392.9 6.2 %copy-start.4 = (f32[1024,1024]{1,0:T(8,128)S(1)}, f32[1024,1024]{1,0:T(8,128)}, u32[]{:S(2)}) copy-start(f32[1024,1024]{1,0:T(8,128)} %copy-done.3) | copy-start | bytes 12582916
  392.9 6.2 %copy-start.22 = (bf16[1024,1024]{1,0:T(8,128)(2,1)S(1)}, bf16[1024,1024]{1,0:T(8,128)(2,1)}, u32[]{:S(2)}) copy-start(bf16[1024,1024]{1,0:T(8,128)(2,1)} %get-tuple-element.58) | copy-start | bytes 6291460
  392.9 9.9 %slice-start = ((s8[8388608]{0:T(1024)(128)(4,1)}), s8[4194304]{0:T(1024)(128)(4,1)S(1)}, s32[]{:S(2)}) async-start(s8[8388608]{0:T(1024)(128)(4,1)} %bitcast.121), calls=%async_computation | async-start | bytes 8388608
  399.1 3.8 copy-start.21
  399.1 3.8 slice-start.1
  589.0 5.4 copy-start.9
  594.3 1.4 copy-start.16
  594.3 2.0 copy-start.15
  594.3 2.7 copy-start.14
  594.3 3.3 copy-start.13
  594.3 4.0 copy-start.12
  594.3 4.8 copy-start.11
